TPU v7x, 32 devices: a whole 2x2x4 slice. The times are simulated.
32 devices in a mesh: rows: 8 (over z, y), seq: 4 (over x, core).
Axes of the slice: x: 2, y: 2, z: 4, core: 2. Of those that a mesh axis runs over, the one named last changes fastest.
Arguments:
- tokens: bfloat16 [16, 1024, 1024], P('rows', 'seq'), may hold values from -6 to 6
- bounds: int32 [16, 4], P('rows'), may hold values from 0 to 1023, as said below
- norm1_gain: float32 [1024], replicated, may hold values from 0.25 to 1.75
- norm1_bias: float32 [1024], replicated, may hold values from -1.5 to 1.5
- w_qkv: bfloat16 [1024, 3072], replicated, may hold values from -0.1875 to 0.1875
- w_proj: bfloat16 [1024, 1024], replicated, may hold values from -1.5 to 1.5
- norm2_gain: float32 [1024], replicated, may hold values from 0.25 to 1.75
- norm2_bias: float32 [1024], replicated, may hold values from -1.5 to 1.5
- w_up: bfloat16 [1024, 4096], replicated, may hold values from -0.1875 to 0.1875
- up_bias: float32 [4096], replicated, may hold values from -1.5 to 1.5
- w_down: bfloat16 [4096, 1024], replicated, may hold values from -0.09375 to 0.09375
- down_bias: float32 [1024], replicated, may hold values from -1.5 to 1.5
- cotangent: bfloat16 [16, 1024, 1024], P('rows', 'seq'), may hold values from -6 to 6
Outputs:
- layer_out: bfloat16 [16, 1024, 1024], P('rows', 'seq')
- grad_tokens: float32 [16, 1024, 1024], P('rows', 'seq')
- grad_norm1_gain: float32 [1024], P(('rows', 'seq'))
- grad_norm1_bias: float32 [1024], P(('rows', 'seq'))
- grad_qkv: float32 [1024, 3072], P(('rows', 'seq'))
- grad_proj: float32 [1024, 1024], P(('rows', 'seq'))
- grad_norm2_gain: float32 [1024], P(('rows', 'seq'))
- grad_norm2_bias: float32 [1024], P(('rows', 'seq'))
- grad_up: float32 [1024, 4096], P(('rows', 'seq'))
- grad_up_bias: float32 [4096], P(('rows', 'seq'))
- grad_down: float32 [4096, 1024], P(('rows', 'seq'))
- grad_down_bias: float32 [1024], P(('rows', 'seq'))
Inputs may be any that keep to these rules, and one draw needn't show every extreme that they name: `bounds`: each row lists the first positions of its 4 documents in increasing order, the first being 0. In every aligned block of 2 rows one row has a document that begins within its first 256 positions and ends within its last 256.
All inputs are finite; a program needn't handle non-finite values.
Results may differ from a plain program's by a relative error of at most 0.007.
Values may be sent and summed in bfloat16 or wider, within the bound.
No kernel may reach another device: no remote copies, remote signals or barrier semaphores. Data moves between devices by JAX's collectives and lax.ppermute only.
A program may use at most 256 MiB of HBM per device.

v0:
```python
import jax
import jax.numpy as jnp
from jax import lax
from jax.sharding import PartitionSpec as P

HEADS = 16


EPS = 1e-05
HIGH = lax.Precision.HIGHEST


def carried_in(array, axis, combine, identity, reverse):
    devices, here = (lax.axis_size(axis), lax.axis_index(axis))
    everything = jax.tree.map(
        lambda part, kind: lax.all_gather(part.astype(kind), axis),
        array,
        (jnp.bfloat16, jnp.bfloat16, jnp.bfloat16),
    )
    start = jax.tree.map(
        lambda part, zero: jnp.broadcast_to(jnp.asarray(zero, part.dtype), part.shape),
        array,
        identity,
    )

    def turn(k, before):
        at = devices - 1 - k if reverse else k
        reached = at > here if reverse else at < here
        new = combine(
            before, jax.tree.map(lambda part, own: part[at].astype(own.dtype), everything, array)
        )
        return jax.tree.map(lambda a, b: jnp.where(reached, a, b), new, before)

    return lax.fori_loop(0, devices, turn, start)


def layer_norm(inputs, gain, bias):
    center = inputs - jnp.mean(inputs, -1, keepdims=True)
    spread = jnp.mean(center * center, -1, keepdims=True)
    return center * lax.rsqrt(spread + EPS) * gain + bias


def doc_ids(bounds, first, count):
    place = first + jnp.arange(count, dtype=jnp.int32)
    hits = (bounds[:, None, :] <= place[None, :, None]).astype(jnp.int32)
    return jnp.sum(hits, -1) - 1


def link(earlier, later):
    carry_on = 1.0 - later[2]
    return (
        later[0] + carry_on[:, None, None, None] * earlier[0],
        later[1] + carry_on[:, None, None] * earlier[1],
        jnp.maximum(earlier[2], later[2]),
    )


def block_weights(query_map, key_map, docs):
    span = docs.shape[1]
    causal = jnp.arange(span)[:, None] >= jnp.arange(span)[None, :]
    same = docs[:, :, None] == docs[:, None, :]
    mask = (causal[None] & same)[:, None].astype(jnp.float32)
    scores = jnp.einsum("rtge,rsge->rgts", query_map, key_map, preferred_element_type=jnp.float32)
    return ((scores * mask).astype(jnp.bfloat16), mask)


def block_state(key_map, values, docs, before):
    last = docs[:, -1]
    keep = (docs == last[:, None]).astype(jnp.bfloat16)[:, :, None, None]
    owned = key_map * keep
    own = jnp.einsum("rsge,rsgf->rgef", owned, values, preferred_element_type=jnp.float32)
    own_sum = jnp.sum(owned.astype(jnp.float32), axis=1)
    flag = (last != before).astype(jnp.float32)
    return (own, own_sum, flag)


def block_output(query_map, values, weights, docs, before, state, state_sum):
    carried = (docs == before[:, None]).astype(jnp.float32)
    query = query_map.astype(jnp.float32)
    numer = jnp.einsum("rgts,rsge->rtge", weights, values, preferred_element_type=jnp.float32)
    numer = numer + carried[:, :, None, None] * jnp.einsum(
        "rtge,rgef->rtgf", query, state, precision=HIGH
    )
    ones = jnp.ones((weights.shape[-1],), jnp.bfloat16)
    denom = jnp.einsum("rgts,s->rtg", weights, ones, preferred_element_type=jnp.float32)
    denom = denom + carried[:, :, None] * jnp.einsum(
        "rtge,rge->rtg", query, state_sum, precision=HIGH
    )
    return (numer / denom[..., None], denom)


def state_grads(query_map, docs, before, outputs, denom, d_out):
    carried = (docs == before[:, None]).astype(jnp.float32)
    d_denom = -jnp.sum(d_out * outputs, -1) / denom
    d_numer = (d_out / denom[..., None]).astype(jnp.bfloat16)
    picked = query_map * carried.astype(jnp.bfloat16)[:, :, None, None]
    d_state = jnp.einsum("rtge,rtgf->rgef", picked, d_numer, preferred_element_type=jnp.float32)
    d_state_sum = jnp.einsum(
        "rtg,rtge->rge",
        carried[:, :, None] * d_denom,
        query_map.astype(jnp.float32),
        precision=HIGH,
    )
    return (d_numer, d_denom, d_state, d_state_sum)


def block_backward(
    query_map,
    key_map,
    values,
    weights,
    mask,
    docs,
    before,
    state,
    state_sum,
    d_numer,
    d_denom,
    d_own,
    d_own_sum,
):
    carried = (docs == before[:, None]).astype(jnp.float32)[:, :, None, None]
    keep = (docs == docs[:, -1:]).astype(jnp.float32)[:, :, None, None]
    d_weights = jnp.einsum("rtge,rsge->rgts", d_numer, values, preferred_element_type=jnp.float32)
    d_weights = d_weights + jnp.transpose(d_denom, (0, 2, 1))[:, :, :, None]
    d_scores = d_weights.astype(jnp.bfloat16) * mask.astype(jnp.bfloat16)
    d_query = jnp.einsum("rgts,rsge->rtge", d_scores, key_map, preferred_element_type=jnp.float32)
    inner = jnp.einsum("rtgf,rgef->rtge", d_numer.astype(jnp.float32), state, precision=HIGH)
    d_query = d_query + carried * (inner + d_denom[:, :, :, None] * state_sum[:, None])
    d_key = jnp.einsum("rgts,rtge->rsge", d_scores, query_map, preferred_element_type=jnp.float32)
    through = jnp.einsum("rsgf,rgef->rsge", values.astype(jnp.float32), d_own, precision=HIGH)
    d_key = d_key + keep * (through + d_own_sum[:, None])
    d_value = jnp.einsum("rgts,rtge->rsge", weights, d_numer, preferred_element_type=jnp.float32)
    d_value = d_value + keep * jnp.einsum(
        "rsge,rgef->rsgf", key_map.astype(jnp.float32), d_own, precision=HIGH
    )
    return (d_query, d_key, d_value)


def local(
    tokens,
    bounds,
    norm1_gain,
    norm1_bias,
    w_qkv,
    w_proj,
    norm2_gain,
    norm2_bias,
    w_up,
    up_bias,
    w_down,
    down_bias,
    cotangent,
):
    rows, span, model = tokens.shape
    head = model // HEADS
    first = lax.axis_index("seq") * span
    docs = doc_ids(bounds, first, span)
    before = doc_ids(bounds, first - 1, 1)[:, 0]
    inputs = tokens.astype(jnp.float32)
    normed1, pull_norm1 = jax.vjp(layer_norm, inputs, norm1_gain, norm1_bias)
    low1 = normed1.astype(jnp.bfloat16)
    mixed = jnp.einsum("rtd,dk->rtk", low1, w_qkv, preferred_element_type=jnp.float32)
    mixed4 = mixed.reshape(rows, span, 3, model)
    query_map = (
        (jax.nn.elu(mixed4[:, :, 0]) + 1.0).astype(jnp.bfloat16).reshape(rows, span, HEADS, head)
    )
    key_map = (
        (jax.nn.elu(mixed4[:, :, 1]) + 1.0).astype(jnp.bfloat16).reshape(rows, span, HEADS, head)
    )
    values = mixed4[:, :, 2].astype(jnp.bfloat16).reshape(rows, span, HEADS, head)
    own, own_sum, flag = block_state(key_map, values, docs, before)
    empty = (jnp.zeros_like(own), jnp.zeros_like(own_sum), jnp.zeros_like(flag))
    state, state_sum, unused = carried_in((own, own_sum, flag), "seq", link, empty, False)
    weights, mask = block_weights(query_map, key_map, docs)
    outputs, denom = block_output(query_map, values, weights, docs, before, state, state_sum)
    attended = outputs.astype(jnp.bfloat16).reshape(rows, span, model)
    middle = inputs + jnp.einsum(
        "rtd,de->rte", attended, w_proj, preferred_element_type=jnp.float32
    )
    normed2, pull_norm2 = jax.vjp(layer_norm, middle, norm2_gain, norm2_bias)
    low2 = normed2.astype(jnp.bfloat16)
    pre = jnp.einsum("rtd,df->rtf", low2, w_up, preferred_element_type=jnp.float32) + up_bias
    active, pull_gelu = jax.vjp(jax.nn.gelu, pre)
    hidden = active.astype(jnp.bfloat16)
    result = (
        middle
        + jnp.einsum("rtf,fd->rtd", hidden, w_down, preferred_element_type=jnp.float32)
        + down_bias
    )
    layer_out = result.astype(jnp.bfloat16)
    d_result = cotangent.astype(jnp.float32)
    grad_down = jnp.einsum("rtf,rtd->fd", hidden, cotangent, preferred_element_type=jnp.float32)
    grad_down_bias = jnp.sum(d_result, (0, 1))
    d_active = jnp.einsum("rtd,fd->rtf", cotangent, w_down, preferred_element_type=jnp.float32)
    d_pre = pull_gelu(d_active)[0].astype(jnp.bfloat16)
    grad_up_bias = jnp.sum(d_pre.astype(jnp.float32), (0, 1))
    grad_up = jnp.einsum("rtd,rtf->df", low2, d_pre, preferred_element_type=jnp.float32)
    d_normed2 = jnp.einsum("rtf,df->rtd", d_pre, w_up, preferred_element_type=jnp.float32)
    d_mid_norm, grad_norm2_gain, grad_norm2_bias = pull_norm2(d_normed2)
    d_middle = d_result + d_mid_norm
    d_branch = d_middle.astype(jnp.bfloat16)
    grad_proj = jnp.einsum("rtd,rte->de", attended, d_branch, preferred_element_type=jnp.float32)
    d_attended = jnp.einsum("rte,de->rtd", d_branch, w_proj, preferred_element_type=jnp.float32)
    d_out = d_attended.reshape(rows, span, HEADS, head)
    d_numer, d_denom, d_state, d_state_sum = state_grads(
        query_map, docs, before, outputs, denom, d_out
    )
    nothing = (jnp.zeros_like(d_state), jnp.zeros_like(d_state_sum), jnp.zeros_like(flag))
    d_own, d_own_sum, unused_flag = carried_in(
        (d_state, d_state_sum, flag), "seq", link, nothing, True
    )
    weights, mask = block_weights(query_map, key_map, docs)
    d_query, d_key, d_value = block_backward(
        query_map,
        key_map,
        values,
        weights,
        mask,
        docs,
        before,
        state,
        state_sum,
        d_numer,
        d_denom,
        d_own,
        d_own_sum,
    )
    d_feats = jnp.stack([d_query, d_key, d_value], 2).reshape(rows, span, 3, model)
    negative = jnp.minimum(mixed4[:, :, :2], 0.0)
    slope = jnp.where(mixed4[:, :, :2] > 0, 1.0, jnp.exp(negative))
    d_mixed = jnp.concatenate([d_feats[:, :, :2] * slope, d_feats[:, :, 2:]], 2)
    d_mixed = d_mixed.reshape(rows, span, 3 * model).astype(jnp.bfloat16)
    grad_qkv = jnp.einsum("rtd,rtk->dk", low1, d_mixed, preferred_element_type=jnp.float32)
    d_normed1 = jnp.einsum("rtk,dk->rtd", d_mixed, w_qkv, preferred_element_type=jnp.float32)
    d_in_norm, grad_norm1_gain, grad_norm1_bias = pull_norm1(d_normed1)
    grad_tokens = d_middle + d_in_norm
    g_qkv, g_proj, g_gain1, g_bias1, g_down, g_down_bias, g_up, g_up_bias, g_gain2, g_bias2 = (
        lax.psum_scatter(grad_qkv, ("rows", "seq"), scatter_dimension=0, tiled=True),
        lax.psum_scatter(grad_proj, ("rows", "seq"), scatter_dimension=0, tiled=True),
        lax.psum_scatter(grad_norm1_gain, ("rows", "seq"), scatter_dimension=0, tiled=True),
        lax.psum_scatter(grad_norm1_bias, ("rows", "seq"), scatter_dimension=0, tiled=True),
        lax.psum_scatter(grad_down, ("rows", "seq"), scatter_dimension=0, tiled=True),
        lax.psum_scatter(grad_down_bias, ("rows", "seq"), scatter_dimension=0, tiled=True),
        lax.psum_scatter(grad_up, ("rows", "seq"), scatter_dimension=0, tiled=True),
        lax.psum_scatter(grad_up_bias, ("rows", "seq"), scatter_dimension=0, tiled=True),
        lax.psum_scatter(grad_norm2_gain, ("rows", "seq"), scatter_dimension=0, tiled=True),
        lax.psum_scatter(grad_norm2_bias, ("rows", "seq"), scatter_dimension=0, tiled=True),
    )
    return (
        layer_out,
        grad_tokens,
        g_gain1,
        g_bias1,
        g_qkv,
        g_proj,
        g_gain2,
        g_bias2,
        g_up,
        g_up_bias,
        g_down,
        g_down_bias,
    )


def solution(mesh):
    in_specs = (
        P("rows", "seq", None),
        P("rows", None),
        P(),
        P(),
        P(),
        P(),
        P(),
        P(),
        P(),
        P(),
        P(),
        P(),
        P("rows", "seq", None),
    )
    out_specs = (
        P("rows", "seq", None),
        P("rows", "seq", None),
        P(("rows", "seq")),
        P(("rows", "seq")),
        P(("rows", "seq"), None),
        P(("rows", "seq"), None),
        P(("rows", "seq")),
        P(("rows", "seq")),
        P(("rows", "seq"), None),
        P(("rows", "seq")),
        P(("rows", "seq"), None),
        P(("rows", "seq")),
    )
    return jax.shard_map(local, mesh=mesh, in_specs=in_specs, out_specs=out_specs, check_vma=False)
```

profile of v0, /device:TPU:0, one launch (start us, length us, event | category | flops | bytes accessed | tf_op | source)
XLA Modules:
  0.0 804.5 jit_solution(14542645575767041482)
XLA Ops:
  9.3 1.4 convert_reduce_fusion.1
  10.7 1.6 fusion.42
  12.4 5.9 fusion.27
  18.4 2.0 fusion.90
  26.1 5.9 all-gather.3
  32.3 5.6 all_gather.34
  38.8 2.5 fusion.46
  44.6 2.7 fusion.93
  47.3 4.1 all-gather.7.cloned.1.call-done
  51.4 6.4 while.34
  51.6 1.4 fusion.141
  53.2 1.4 fusion.141
  54.7 1.4 fusion.141
  56.3 1.4 fusion.141
  57.8 1.9 fusion.94
  59.7 3.4 fusion.91
  63.1 1.4 fusion.92
  65.3 7.2 fusion.23
  72.5 13.1 %convert_reduce_fusion = (f32[4096]{0:T(1024)S(1)}, bf16[2,256,4096]{2,1,0:T(8,128)(2,1)S(1)}) fusion(f32[2,256,4096]{2,1,0:T(8,128)} %fusion.23, f32[4096]{0:T(1024)S(1)} %copy-done.35, bf16[2,256,1024]{2,1,0:T(8,128)(2,1)S(1)} %copy-done.25, bf16[4096,1024]{1,0:T(8,128)(2,1)} %param.27), kind=kOutput, calls=%fused_computation.35 | convolution fusion | flops 4343197696 | bytes 22052864 | tf_op jit(solution)/shard_map/rtd,fd->rtf/dot_general | solution.py:195
  85.6 9.0 %multiply_reduce_fusion = (f32[1024]{0:T(1024)S(1)}, f32[2,256]{1,0:T(2,128)S(1)}, f32[1024]{0:T(1024)S(1)}, f32[2,256,1024]{2,1,0:T(8,128)S(1)}) fusion(f32[2,256,1024]{2,1,0:T(8,128)S(1)} %get-tuple-element.498, f32[2,256]{1,0:T(2,128)S(1)} %fusion.79, f32[2,256]{1,0:T(2,128)S(1)} %broadcast_multiply_fusion, f32[1024]{0:T(1024)S(1)} %copy-done.34, ...), kind=kOutput, calls=%fused_computation.91 | convolution fusion | flops 4299159040 | bytes 16795648 | tf_op jit(solution)/shard_map/rtf,df->rtd/dot_general | solution.py:199
  96.6 1.3 multiply_reduce_fusion.1
  100.5 4.8 convolution_bitcast_fusion.3
  106.3 5.2 all-gather.2
  111.5 3.7 fusion.31
  115.2 1.4 fusion.95
  116.6 2.5 fusion.54
  119.2 2.2 fusion.97
  121.4 2.2 fusion.96
  123.6 6.2 while.35
  123.7 1.4 fusion.144
  125.2 1.4 fusion.144
  126.8 1.4 fusion.144
  128.3 1.4 fusion.144
  129.9 2.9 add_convert_fusion.1
  134.3 3.2 fusion.32
  137.9 1.6 copy-done.28
  139.5 6.9 convolution_bitcast_fusion.2
  146.5 1.5 copy-done.17
  148.0 10.8 %convolution_bitcast_fusion.1 = f32[1024,4096]{1,0:T(8,128)} fusion(bf16[2,256,4096]{2,1,0:T(8,128)(2,1)} %copy-done.39, f32[2,256,1024]{2,1,0:T(8,128)S(1)} %copy-done.17, f32[1024]{0:T(1024)S(1)} %copy-done.37, f32[1024]{0:T(1024)S(1)} %copy-done.34, f32[2,256]{1,0:T(2,128)S(1)} %fusion.79, f32[2,256]{1,0:T(2,128)S(1)} %broadcast_multiply_fusion), kind=kOutput, calls=%fused_computation.19 | convolution fusion | flops 4297588736 | bytes 23080960 | tf_op jit(solution)/shard_map/rtd,rtf->df/dot_general | solution.py:198
  158.9 15.6 %convolution_bitcast_fusion = f32[4096,1024]{1,0:T(8,128)} fusion(bf16[2,256,1024]{2,1,0:T(8,128)(2,1)} %param.29, f32[2,256,4096]{2,1,0:T(8,128)} %fusion.23, f32[4096]{0:T(1024)S(1)} %copy-done.35), kind=kOutput, calls=%fused_computation.18 | convolution fusion | flops 4315938816 | bytes 26230784 | tf_op jit(solution)/shard_map/rtf,rtd->fd/dot_general | solution.py:193
  175.2 12.4 %add_convert_fusion.2 = bf16[2,256,1024]{2,1,0:T(8,128)(2,1)} fusion(f32[2,256,1024]{2,1,0:T(8,128)S(1)} %copy-done.17, bf16[4096,1024]{1,0:T(8,128)(2,1)} %param.27, f32[1024]{0:T(1024)S(1)} %copy-done.38, f32[2,256,4096]{2,1,0:T(8,128)} %fusion.23, f32[4096]{0:T(1024)S(1)} %copy-done.35), kind=kOutput, calls=%fused_computation.98 | convolution fusion | flops 4317511680 | bytes 19943424 | tf_op jit(solution)/shard_map/rtf,fd->rtd/dot_general | solution.py:188
  187.6 6.2 fusion.86
  195.7 2.1 convert_reduce_fusion.2
  197.8 40.5 %all-reduce.6 = (f32[1024]{0:T(1024)S(1)}, f32[1024]{0:T(1024)S(1)}, f32[1024]{0:T(1024)S(1)}, f32[1024]{0:T(1024)S(1)}, f32[4096]{0:T(1024)S(1)}, /*index=5*/f32[1024]{0:T(1024)S(1)}) all-reduce(f32[1024]{0:T(1024)S(1)} %get-tuple-element.438, ...), channel_id=5, replica_groups=mesh['rows'=8,'seq'=4] {'rows','seq'}, use_global_device_ids=true, to_apply=%region_17.18.clone | all-reduce | flops 9216 | bytes 73728
  241.7 25.5 %reduce-scatter.7.cloned.1.call-done = f32[32,1024]{1,0:T(8,128)} async-done(((f32[1024,1024]{1,0:T(8,128)}), f32[32,1024]{1,0:T(8,128)}) %reduce-scatter.7.cloned.1.call-update) | async-done | bytes 131088 | tf_op jit(solution)/shard_map/reduce_scatter | solution.py:240
  267.2 157.8 %reduce-scatter.5.cloned.1.call-done = f32[32,3072]{1,0:T(8,128)} async-done(((f32[1024,3072]{1,0:T(8,128)}), f32[32,3072]{1,0:T(8,128)}) %reduce-scatter.5.cloned.1.call-update) | async-done | bytes 393232 | tf_op jit(solution)/shard_map/reduce_scatter | solution.py:239
  425.0 184.8 %reduce-scatter.9.cloned.1.call-done = f32[32,4096]{1,0:T(8,128)} async-done(((f32[1024,4096]{1,0:T(8,128)}), f32[32,4096]{1,0:T(8,128)}) %reduce-scatter.9.cloned.1.call-update) | async-done | bytes 524304 | tf_op jit(solution)/shard_map/reduce_scatter | solution.py:245
  609.8 187.4 %reduce-scatter.11.cloned.1.call-done = f32[128,1024]{1,0:T(8,128)} async-done(((f32[4096,1024]{1,0:T(8,128)}), f32[128,1024]{1,0:T(8,128)}) %reduce-scatter.11.cloned.1.call-update) | async-done | bytes 524304 | tf_op jit(solution)/shard_map/reduce_scatter | solution.py:243
  (162 shorter events, 27.2 us)
Async XLA Ops:
  7.2 55.9 %copy-start = (bf16[1024,1024]{1,0:T(8,128)(2,1)S(1)}, bf16[1024,1024]{1,0:T(8,128)(2,1)}, u32[]{:S(2)}) copy-start(bf16[1024,1024]{1,0:T(8,128)(2,1)} %param.22) | copy-start | bytes 6291460
  7.2 5.2 copy-start.7
  7.2 5.2 copy-start.36
  7.2 5.2 copy-start.33
  7.2 44.2 %all-gather.7.cloned.1.call-start = ((), (), s32[]{:S(2)}) async-start(), calls=%async_computation.8 | async-start | bytes 2621440 | tf_op jit(solution)/shard_map/all_gather | solution.py:16
  12.4 6.0 copy-start.31
  18.4 3.3 copy-start.13
  22.8 1.0 copy-start.20
  23.7 1.0 copy-start.4
  25.9 97.7 %all-gather.9.cloned.1.call-start = ((), (), s32[]{:S(2)}) async-start(), calls=%async_computation.9 | async-start | bytes 2621440 | tf_op jit(solution)/shard_map/all_gather | solution.py:16
  32.3 8.9 %copy-start.5 = (bf16[2,256,16,64]{1,3,2,0:T(8,128)(2,1)S(1)}, bf16[2,256,16,64]{1,3,2,0:T(8,128)(2,1)}, u32[]{:S(2)}) copy-start(bf16[2,256,16,64]{1,3,2,0:T(8,128)(2,1)} %copy-done.4) | copy-start | bytes 3145732
  41.2 1.3 copy-start.10
  42.6 2.0 copy-start.2
  42.6 2.0 copy-start.21
  57.8 7.1 slice-start
  59.7 3.4 copy-start.8
  59.7 5.2 slice-start.1
  63.1 1.4 copy-start.30
  64.5 30.1 %copy-start.16 = (f32[2,256,1024]{2,1,0:T(8,128)}, f32[2,256,1024]{2,1,0:T(8,128)S(1)}, u32[]{:S(2)}) copy-start(f32[2,256,1024]{2,1,0:T(8,128)S(1)} %get-tuple-element.498) | copy-start | bytes 6291460
  64.5 0.7 copy-start.34
  64.5 0.8 copy-start.37
  65.3 7.2 copy-start.25
  65.3 7.2 copy-start.35
  85.6 9.0 %copy-start.39 = (bf16[2,256,4096]{2,1,0:T(8,128)(2,1)}, bf16[2,256,4096]{2,1,0:T(8,128)(2,1)S(1)}, u32[]{:S(2)}) copy-start(bf16[2,256,4096]{2,1,0:T(8,128)(2,1)S(1)} %get-tuple-element.504) | copy-start | bytes 12582916
  95.3 1.4 copy-start.14
  96.6 1.3 copy-start.27
  98.0 1.3 copy-start.11
  98.3 7.0 copy-start.18
  100.5 166.8 %reduce-scatter.7.cloned.1.call-start = ((), (), s32[]{:S(2)}) async-start(), calls=%async_computation.5 | async-start | bytes 4325376 | tf_op jit(solution)/shard_map/reduce_scatter | solution.py:240
  105.3 319.7 %reduce-scatter.5.cloned.1.call-start = ((), (), s32[]{:S(2)}) async-start(), calls=%async_computation.4 | async-start | bytes 12976128 | tf_op jit(solution)/shard_map/reduce_scatter | solution.py:239
  111.5 3.7 copy-start.6
  115.2 1.4 copy-start.19
  116.6 2.6 copy-start.3
  119.2 2.2 copy-start.12
  129.8 2.9 copy-start.22
  129.9 2.9 copy-start.24
  132.8 1.6 copy-start.23
  137.6 2.0 copy-start.9
  137.9 1.7 copy-start.28
  146.5 1.6 copy-start.17
  146.5 463.3 %reduce-scatter.9.cloned.1.call-start = ((), (), s32[]{:S(2)}) async-start(), calls=%async_computation.6 | async-start | bytes 17301504 | tf_op jit(solution)/shard_map/reduce_scatter | solution.py:245
  158.8 638.3 %reduce-scatter.11.cloned.1.call-start = ((), (), s32[]{:S(2)}) async-start(), calls=%async_computation.7 | async-start | bytes 17301504 | tf_op jit(solution)/shard_map/reduce_scatter | solution.py:243
  174.5 0.7 copy-start.38
  175.2 12.4 %copy-start.29 = (bf16[2,256,3,1024]{1,3,2,0:T(8,128)(2,1)S(1)}, bf16[2,256,3,1024]{1,3,2,0:T(8,128)(2,1)}, u32[]{:S(2)}) copy-start(bf16[2,256,3,1024]{1,3,2,0:T(8,128)(2,1)} %copy-done.28) | copy-start | bytes 9437188
  187.6 6.2 copy-start.32
  193.8 1.6 copy-start.15
  193.8 1.8 copy-start.26
  195.7 601.5 %copy-start.1 = (bf16[1024,1024]{1,0:T(8,128)(2,1)S(1)}, bf16[1024,1024]{1,0:T(8,128)(2,1)}, u32[]{:S(2)}) copy-start(bf16[1024,1024]{1,0:T(8,128)(2,1)} %param.22) | copy-start | bytes 6291460
Sparse Core Ops, SparseCore 0:
  26.1 25.2 all-gather.6
  100.6 22.6 all-gather.8
  126.1 141.0 reduce-scatter.6
  273.7 151.2 reduce-scatter.4
  427.8 181.8 reduce-scatter.8
  612.6 184.5 reduce-scatter.10
where the time goes:
time: 813 us; the launch traced here: 804 us
  waiting for transfers between devices  560 us (69%)
  matrix products  125 us (15%)
  blocking collectives  57.2 us (7%)
  other arithmetic  30.9 us (4%)
  local copies, waits for them, and re-layouts  16.4 us (2%)
  between operations  15.2 us (2%)
    reduce_scatter x1, waiting for transfers between devices, local(): lax.psum_scatter(grad_down, ('rows', 'seq'), scatter_dimension=0, tiled=T...  187 us
    reduce_scatter x1, waiting for transfers between devices, local(): lax.psum_scatter(grad_up, ('rows', 'seq'), scatter_dimension=0, tiled=True)  185 us
    reduce_scatter x1, waiting for transfers between devices, local(): lax.psum_scatter(grad_qkv, ('rows', 'seq'), scatter_dimension=0, tiled=True)  158 us
    unnamed x1, blocking collectives  40.5 us
    reduce_scatter x1, waiting for transfers between devices, local(): lax.psum_scatter(grad_proj, ('rows', 'seq'), scatter_dimension=0, tiled=T...  25.5 us
    all_gather x3, blocking collectives, carried_in(): lax.all_gather(part.astype(kind), axis)  16.7 us
  transfers between devices with their start and end apart: 6, of which 5 were waited for; matrix products, arithmetic and copies ran while one was open for 12% of the time, Pallas kernels for 0%

commit v1 on v0

v1 whole, which is shorter than its diff:
```python
import functools

import jax
import jax.numpy as jnp
from jax import lax
from jax.experimental import pallas as pl
from jax.experimental.pallas import tpu as pltpu
from jax.sharding import PartitionSpec as P

HEADS = 16
EPS = 1e-05
BF, F32 = jnp.bfloat16, jnp.float32
AXES = ("rows", "seq")
SUMS = 64
DEPTH = 80
TILE = 512


def dot(a, b):
    return jnp.dot(a, b, preferred_element_type=F32)


def dot_nt(a, b):
    return lax.dot_general(a, b, (((1,), (1,)), ((), ())), preferred_element_type=F32)


def dot_tn(a, b):
    return lax.dot_general(a, b, (((0,), (0,)), ((), ())), preferred_element_type=F32)


def iota(shape, dim):
    return lax.broadcasted_iota(jnp.int32, shape, dim)


def full(shape):
    zeros = (0,) * len(shape)
    return pl.BlockSpec(shape, lambda *unused: zeros)


SMEM = pl.BlockSpec(memory_space=pltpu.SMEM)


def kernel_call(body, args, specs, outs, out_specs, grid, scratch=(), after=(), flops=0, table=None):
    lead = 0 if table is None else 1
    n_in, n_after = lead + len(args), len(after)

    def wrapped(*refs):
        body(*refs[:n_in], *refs[n_in + n_after :])

    shapes = [jax.ShapeDtypeStruct(s, d) for s, d in outs]
    moved = sum(a.size * a.dtype.itemsize for a in args)
    moved += sum(s.size * s.dtype.itemsize for s in shapes)
    every = [*specs, *[pl.BlockSpec(memory_space=pl.ANY)] * n_after]
    common = dict(
        out_shape=shapes,
        compiler_params=pltpu.CompilerParams(vmem_limit_bytes=50 << 20),
        cost_estimate=pl.CostEstimate(flops=flops, bytes_accessed=moved, transcendentals=0),
    )
    if table is None:
        run = pl.pallas_call(
            wrapped, grid=grid, in_specs=every, out_specs=out_specs, scratch_shapes=scratch, **common
        )
        return run(*args, *after)
    spec = pltpu.PrefetchScalarGridSpec(
        num_scalar_prefetch=1, grid=grid, in_specs=every, out_specs=out_specs, scratch_shapes=scratch
    )
    return pl.pallas_call(wrapped, grid_spec=spec, **common)(table, *args, *after)


def normal(x):
    center = x - jnp.mean(x, -1, keepdims=True)
    root = lax.rsqrt(jnp.mean(center * center, -1, keepdims=True) + EPS)
    return center * root, root


def norm_grad(e, x, gain):
    hat, root = normal(x)
    g = e * gain
    back = root * (g - jnp.mean(g, -1, keepdims=True) - hat * jnp.mean(g * hat, -1, keepdims=True))
    return back, jnp.sum(e * hat, 0, keepdims=True), jnp.sum(e, 0, keepdims=True)


def feature(u):
    return jnp.where(u > 0, u + 1.0, jnp.exp(jnp.minimum(u, 0.0)))


def keep_from(lb, row, span):
    last = 0 - span
    for k in range(lb.shape[1]):
        last = jnp.where(lb[row, k] < span, jnp.maximum(last, lb[row, k]), last)
    return last


def carry_to(lb, row, span):
    end = span
    for k in range(lb.shape[1]):
        end = jnp.where(lb[row, k] >= 0, jnp.minimum(end, lb[row, k]), end)
    return end


def block_mask(lb, row, span):
    t, s = iota((span, span), 0), iota((span, span), 1)
    ok = s <= t
    for k in range(lb.shape[1]):
        ok = ok & ((lb[row, k] > t) | (s >= lb[row, k]))
    return ok.astype(F32)


def pack_state(m):
    half = m.shape[0] // 2
    return jnp.where(iota((half, m.shape[1]), 1) < half, m[:half], m[half:])


def unpack_state(c):
    half = c.shape[0]
    left = iota(c.shape, 1) < half
    return jnp.concatenate([jnp.where(left, c, 0.0), jnp.where(left, 0.0, c)], 0)


def split(x):
    hi = x.astype(BF)
    return hi, (x - hi.astype(F32)).astype(BF)


def head_ones(lanes=128):
    half = lanes // 2
    return ((iota((lanes, lanes), 0) < half) == (iota((lanes, lanes), 1) < half)).astype(BF)


def head_sum(x):
    hi, lo = split(x)
    ones = head_ones(x.shape[1])
    return dot(jnp.concatenate([hi, lo], 1), jnp.concatenate([ones, ones], 0))


def dot_split(a, m):
    hi, lo = split(m)
    return dot(jnp.concatenate([a, a], 1), jnp.concatenate([hi, lo], 0))


def keys_values(lb, tokens, gain, bias, w_qkv, span, after=()):
    count, model = tokens.shape
    rows, width = count // span, 256

    def body(lb, x, g, b, wk, wv, n1, km, v, own):
        @pl.when(pl.program_id(0) == 0)
        def _():
            n1[...] = (normal(x[...].astype(F32))[0] * g[...] + b[...]).astype(BF)

        n = n1[...]
        key = feature(dot(n, wk[...])).astype(BF)
        val = dot(n, wv[...]).astype(BF)
        km[...], v[...] = key, val
        for r in range(rows):
            part = slice(r * span, (r + 1) * span)
            kept = iota((span, width), 0) >= keep_from(lb, r, span)
            owned = jnp.where(kept, key[part], jnp.zeros((), BF))
            for p in range(width // 128):
                lanes = slice(p * 128, (p + 1) * 128)
                m = dot_tn(owned[:, lanes], val[part, lanes])
                own[r, p, 0:SUMS] = pack_state(m).astype(BF)
                total = jnp.sum(owned[:, lanes].astype(F32), 0, keepdims=True)
                own[r, p, SUMS:DEPTH] = jnp.broadcast_to(total, (DEPTH - SUMS, 128)).astype(BF)

    steps = model // width
    tile = pl.BlockSpec((count, width), lambda j: (0, j))
    return kernel_call(
        body,
        (lb, tokens, gain, bias, w_qkv, w_qkv),
        [
            SMEM,
            full((count, model)),
            full((1, model)),
            full((1, model)),
            pl.BlockSpec((model, width), lambda j: (0, steps + j)),
            pl.BlockSpec((model, width), lambda j: (0, 2 * steps + j)),
        ],
        [
            ((count, model), BF),
            ((count, model), BF),
            ((count, model), BF),
            ((rows, model // 128, DEPTH, 128), BF),
        ],
        [
            full((count, model)),
            tile,
            tile,
            pl.BlockSpec((rows, width // 128, DEPTH, 128), lambda j: (0, j, 0, 0)),
        ],
        (steps,),
        after=after,
        flops=4 * count * model * model,
    )


def queries(normed, w_qkv, after=()):
    count, model = normed.shape

    def body(n, w, q):
        q[...] = feature(dot(n[...], w[...])).astype(BF)

    tile = pl.BlockSpec((count, TILE), lambda j: (0, j))
    return kernel_call(
        body,
        (normed, w_qkv),
        [full((count, model)), pl.BlockSpec((model, TILE), lambda j: (0, j))],
        [((count, model), BF)],
        [tile],
        (model // TILE,),
        after=after,
        flops=2 * count * model * model,
    )[0]


def active_grads(cotangent, w_down, after=()):
    count, model = cotangent.shape
    ff = w_down.shape[0]

    def body(c, w, out):
        out[...] = dot_nt(c[...], w[...])

    return kernel_call(
        body,
        (cotangent, w_down),
        [full((count, model)), pl.BlockSpec((TILE, model), lambda j: (j, 0))],
        [((count, ff), F32)],
        [pl.BlockSpec((count, TILE), lambda j: (0, j))],
        (ff // TILE,),
        after=after,
        flops=2 * count * model * ff,
    )[0]


def attend_inside(lb, query, key, values, span, after=()):
    count, model = query.shape
    width = 512

    def body(lb, q_ref, k_ref, v_ref, numer, denom, mask):
        row = pl.program_id(0)

        @pl.when(pl.program_id(1) == 0)
        def _():
            mask[...] = block_mask(lb, row, span)

        left = iota((span, 128), 1) < 64
        zero = jnp.zeros((), BF)
        for p in range(width // 128):
            lanes = slice(p * 128, (p + 1) * 128)
            q, k, v = q_ref[:, lanes], k_ref[:, lanes], v_ref[:, lanes]
            total = 0.0
            for e in range(2):
                mine = left if e == 0 else ~left
                scores = dot_nt(jnp.where(mine, q, zero), k)
                weights = (scores * mask[...]).astype(BF)
                both = jnp.concatenate([jnp.where(mine, v, zero), mine.astype(BF)], 1)
                total = total + dot(weights, both)
            numer[:, lanes] = total[:, :128]
            denom[:, lanes] = total[:, 128:]

    tile = pl.BlockSpec((span, width), lambda r, h: (r, h))
    return kernel_call(
        body,
        (lb, query, key, values),
        [SMEM, tile, tile, tile],
        [((count, model), F32)] * 2,
        [tile, tile],
        (count // span, model // width),
        scratch=[pltpu.VMEM((span, span), F32)],
        after=after,
        flops=16 * count * span * model // 4,
    )


def attend_join(lb, state, query, numer, denom, tokens, w_proj, gain, bias, span, after=()):
    count, model = query.shape
    step = 128
    pairs = model // 128

    def body(lb, st, q_ref, num_ref, den_ref, x, w, g, b, att, rden, middle, n2):
        i = pl.program_id(0)
        row = i * step // span
        place = iota((step, 128), 0) + lax.rem(i * step, span)
        carried = place < carry_to(lb, row, span)
        for p in range(pairs):
            lanes = slice(p * 128, (p + 1) * 128)
            q = jnp.where(carried, q_ref[:, lanes], jnp.zeros((), BF))
            num = num_ref[:, lanes] + dot_split(q, unpack_state(st[0, p, 0:SUMS]))
            den = den_ref[:, lanes] + head_sum(q.astype(F32) * st[0, p, SUMS : SUMS + 1])
            inv = 1.0 / den
            rden[:, lanes] = inv
            att[:, lanes] = (num * inv).astype(BF)
        mid = x[...].astype(F32) + dot(att[...], w[...])
        middle[...] = mid
        n2[...] = (normal(mid)[0] * g[...] + b[...]).astype(BF)

    tile = pl.BlockSpec((step, model), lambda i: (i, 0))
    return kernel_call(
        body,
        (lb, state, query, numer, denom, tokens, w_proj, gain, bias),
        [
            SMEM,
            pl.BlockSpec((1, pairs, DEPTH, 128), lambda i: (i * step // span, 0, 0, 0)),
            tile,
            tile,
            tile,
            tile,
            full(w_proj.shape),
            full((1, model)),
            full((1, model)),
        ],
        [((count, model), BF), ((count, model), F32), ((count, model), F32), ((count, model), BF)],
        [tile] * 4,
        (count // step,),
        after=after,
        flops=2 * count * model * (model + 512),
    )


def expand(normed, w_up, up_bias, d_active, after=()):
    count, model = normed.shape
    ff = w_up.shape[1]
    c0, c1 = 0.7978845608028654, 0.7978845608028654 * 0.044715

    def body(n, w, b, da, hid, hid_t, dp, total):
        for part in range(2):
            rows = slice(part * count // 2, (part + 1) * count // 2)
            u = dot(n[rows, :], w[...]) + b[...]
            sq = u * u
            t = jnp.tanh(u * (c0 + c1 * sq))
            half = 0.5 * u
            h = (half + half * t).astype(BF)
            hid[rows, :] = h
            hid_t[:, rows] = h.T
            slope = (0.5 + 0.5 * t) + half * (1.0 - t * t) * (c0 + 3.0 * c1 * sq)
            d = (slope * da[rows, :]).astype(BF)
            dp[rows, :] = d
            part_sum = jnp.sum(d.astype(F32), 0, keepdims=True)
            total[...] = part_sum if part == 0 else total[...] + part_sum

    tile = pl.BlockSpec((count, TILE), lambda j: (0, j))
    vec = pl.BlockSpec((1, TILE), lambda j: (0, j))
    return kernel_call(
        body,
        (normed, w_up, up_bias, d_active),
        [full((count, model)), pl.BlockSpec((model, TILE), lambda j: (0, j)), vec, tile],
        [((count, ff), BF), ((ff, count), BF), ((count, ff), BF), ((1, ff), F32)],
        [tile, pl.BlockSpec((TILE, count), lambda j: (j, 0)), tile, vec],
        (ff // TILE,),
        after=after,
        flops=2 * count * model * ff,
    )


def turned(x, place, shards, after=()):
    count, model = x.shape
    deep = model // shards

    def body(place, x, out):
        for j in range(model // 128):
            t = x[:, j * 128 : (j + 1) * 128].T
            for k in range(128 // deep):
                at = pl.multiple_of(place[j * (128 // deep) + k] * deep, deep)
                out[pl.ds(at, deep), :] = t[k * deep : (k + 1) * deep]

    return kernel_call(
        body, (place, x), [SMEM, full(x.shape)], [((model, count), BF)], [full((model, count))], (1,), after=after
    )[0]


def weight_grad(lhs_t, rhs, block_of, steps, table, got=None, after=()):
    deep, count = lhs_t.shape
    half = deep // 2
    block = (*(None,) * (rhs.ndim - 2), count, TILE)
    in_specs = [full(lhs_t.shape), pl.BlockSpec(block, lambda j, t: block_of(j, t))]
    flops = 2 * deep * count * TILE * steps
    if got is None:

        shards = table.shape[0] - 1
        rows = deep // shards

        def body(table, a, b, out):
            total = dot(a[...], b[...]).astype(BF)
            for j in range(shards):
                at = (j & 0b01010) | (j >> 4 & 1) << 2 | (j >> 2 & 1) << 4 | (~j & 1)
                out[at * rows : (at + 1) * rows, :] = total[j * rows : (j + 1) * rows]

        return kernel_call(
            body,
            (lhs_t, rhs),
            in_specs,
            [((deep, TILE * steps), BF)],
            [pl.BlockSpec((deep, TILE), lambda j, t: (0, j))],
            (steps,),
            after=after,
            flops=flops,
            table=table,
        )[0]

    def body(table, a, b, g, send, keep):
        total = dot(a[...], b[...]) + g[...].astype(F32)
        send[...] = total[:half].astype(BF)
        keep[...] = total[half:].astype(BF)

    return kernel_call(
        body,
        (lhs_t, rhs, got),
        [*in_specs, pl.BlockSpec((deep, TILE), lambda j, t: (0, j))],
        [((half, TILE * steps), BF)] * 2,
        [pl.BlockSpec((half, TILE), lambda j, t: (0, j))] * 2,
        (steps,),
        after=after,
        flops=flops,
        table=table,
    )


def down_grad(hidden_t, cotangent, width, column_of, table, got=None, after=()):
    ff, count = hidden_t.shape
    shards = table.shape[0] - 1
    deep = ff // shards
    per = TILE // deep
    steps = ff // TILE
    half = steps // 2

    def piece(k):
        return pl.BlockSpec((deep, count), lambda i, t: (t[per * i + k], 0))

    in_specs = [piece(k) for k in range(per)]
    in_specs += [pl.BlockSpec((count, width), lambda i, t: (0, column_of(t)))]
    args = (*[hidden_t] * per, cotangent)
    flops = 2 * ff * count * width

    def product(refs):
        return dot(jnp.concatenate([r[...] for r in refs[:per]], 0), refs[per][...])

    if got is None:

        def body(table, *refs):
            refs[-1][...] = product(refs).astype(BF)

        return kernel_call(
            body,
            args,
            in_specs,
            [((ff, width), BF)],
            [pl.BlockSpec((TILE, width), lambda i, t: (i, 0))],
            (steps,),
            after=after,
            flops=flops,
            table=table,
        )[0]

    def body(table, *refs):
        g, send, keep = refs[per + 1 :]
        total = (product(refs) + g[...].astype(F32)).astype(BF)

        @pl.when(pl.program_id(0) < half)
        def _():
            send[...] = total

        @pl.when(pl.program_id(0) >= half)
        def _():
            keep[...] = total

    return kernel_call(
        body,
        (*args, got),
        [*in_specs, pl.BlockSpec((TILE, width), lambda i, t: (i, 0))],
        [((ff // 2, width), BF)] * 2,
        [
            pl.BlockSpec((TILE, width), lambda i, t: (jnp.minimum(i, half - 1), 0)),
            pl.BlockSpec((TILE, width), lambda i, t: (jnp.maximum(i - half, 0), 0)),
        ],
        (steps,),
        after=after,
        flops=flops,
        table=table,
    )


def second_norm_grads(d_pre, w_up, middle, cotangent, gain, after=()):
    count, ff = d_pre.shape
    model = w_up.shape[0]
    steps = ff // TILE

    def body(d, w, mid, cot, g, d_mid, branch, g_gain, g_bias, g_down, total):
        j = pl.program_id(0)

        @pl.when(j == 0)
        def _():
            total[...] = dot_nt(d[...], w[...])

        @pl.when(j > 0)
        def _():
            total[...] += dot_nt(d[...], w[...])

        @pl.when(j == steps - 1)
        def _():
            back, g_gain[...], g_bias[...] = norm_grad(total[...], mid[...], g[...])
            c = cot[...].astype(F32)
            g_down[...] = jnp.sum(c, 0, keepdims=True)
            out = c + back
            d_mid[...] = out
            branch[...] = out.astype(BF)

    vec = ((1, model), F32)
    return kernel_call(
        body,
        (d_pre, w_up, middle, cotangent, gain),
        [
            pl.BlockSpec((count, TILE), lambda j: (0, j)),
            pl.BlockSpec((model, TILE), lambda j: (0, j)),
            full((count, model)),
            full((count, model)),
            full((1, model)),
        ],
        [((count, model), F32), ((count, model), BF), vec, vec, vec],
        [full((count, model)), full((count, model)), *[full((1, model))] * 3],
        (steps,),
        scratch=[pltpu.VMEM((count, model), F32)],
        after=after,
        flops=2 * count * model * ff,
    )


def mixer_grads(lb, branch, w_proj, attended, rden, query, span, after=()):
    count, model = branch.shape
    rows, pairs = count // span, model // 128

    def body(lb, br, w, att, rd, q_ref, dn, dd, own):
        d_att = dot_nt(br[...], w[...])
        carried = iota((span, 128), 0) < carry_to(lb, pl.program_id(0), span)
        for p in range(pairs):
            lanes = slice(p * 128, (p + 1) * 128)
            d, inv = d_att[:, lanes], rd[:, lanes]
            d_den = -head_sum(d * att[:, lanes].astype(F32)) * inv
            d_num = (d * inv).astype(BF)
            dn[:, lanes], dd[:, lanes] = d_num, d_den
            q = jnp.where(carried, q_ref[:, lanes], jnp.zeros((), BF))
            own[0, p, 0:SUMS] = pack_state(dot_tn(q, d_num)).astype(BF)
            total = jnp.sum(d_den * q.astype(F32), 0, keepdims=True)
            own[0, p, SUMS:DEPTH] = jnp.broadcast_to(total, (DEPTH - SUMS, 128)).astype(BF)

    tile = pl.BlockSpec((span, model), lambda r: (r, 0))
    return kernel_call(
        body,
        (lb, branch, w_proj, attended, rden, query),
        [SMEM, tile, full(w_proj.shape), tile, tile, tile],
        [((count, model), BF), ((count, model), F32), ((rows, pairs, DEPTH, 128), BF)],
        [tile, tile, pl.BlockSpec((1, pairs, DEPTH, 128), lambda r: (r, 0, 0, 0))],
        (rows,),
        after=after,
        flops=2 * count * model * (model + 512),
    )


def attend_back(lb, query, key, values, d_num, d_den, state, d_own, span, after=()):
    count, model = query.shape
    width = 512
    half = width // 128

    def body(lb, q_ref, k_ref, v_ref, dn_ref, dd_ref, st, own, out, mask, mask_t):
        row = pl.program_id(0)

        @pl.when(pl.program_id(1) == 0)
        def _():
            m = block_mask(lb, row, span)
            mask[...] = m
            mask_t[...] = m.T

        lane = iota((span, 128), 1)
        left = lane < 64
        place = iota((span, 128), 0)
        carried = place < carry_to(lb, row, span)
        kept = place >= keep_from(lb, row, span)
        zero = jnp.zeros((), BF)
        for p in range(half):
            lanes = slice(p * 128, (p + 1) * 128)
            q, k, v = q_ref[:, lanes], k_ref[:, lanes], v_ref[:, lanes]
            dn, dd = dn_ref[:, lanes], dd_ref[:, lanes]
            hi, lo = split(dd)
            v_ones = jnp.concatenate([v, jnp.ones_like(v)], 1)
            dq = dk = dv = 0.0
            for e in range(2):
                mine = left if e == 0 else ~left
                at = 64 * e
                qm, dnm = jnp.where(mine, q, zero), jnp.where(mine, dn, zero)
                extra = jnp.where(lane == at, hi, jnp.where(lane == at + 1, lo, zero))
                dn_den = jnp.concatenate([dnm, extra], 1)
                ds = (dot_nt(dn_den, v_ones).astype(BF).astype(F32) * mask[...]).astype(BF)
                ds_t = (dot_nt(v_ones, dn_den).astype(BF).astype(F32) * mask_t[...]).astype(BF)
                w_t = (dot_nt(k, qm) * mask_t[...]).astype(BF)
                dq = dq + dot(ds, jnp.where(mine, k, zero))
                dk = dk + dot(ds_t, qm)
                dv = dv + dot(w_t, dnm)
            s = unpack_state(st[0, p, 0:SUMS])
            o = unpack_state(own[0, p, 0:SUMS])
            s_hi, s_lo = split(s)
            o_hi, o_lo = split(o)
            through_s = dot_nt(jnp.concatenate([dn, dn], 1), jnp.concatenate([s_hi, s_lo], 1))
            through_o = dot_nt(jnp.concatenate([v, v], 1), jnp.concatenate([o_hi, o_lo], 1))
            dq = dq + jnp.where(carried, through_s + dd * st[0, p, SUMS : SUMS + 1], 0.0)
            dk = dk + jnp.where(kept, through_o + own[0, p, SUMS : SUMS + 1], 0.0)
            dv = dv + jnp.where(kept, dot(jnp.concatenate([k, k], 1), jnp.concatenate([o_hi, o_lo], 0)), 0.0)
            out[0, :, lanes] = (dq * jnp.minimum(q.astype(F32), 1.0)).astype(BF)
            out[1, :, lanes] = (dk * jnp.minimum(k.astype(F32), 1.0)).astype(BF)
            out[2, :, lanes] = dv.astype(BF)

    tile = pl.BlockSpec((span, width), lambda r, h: (r, h))
    states = pl.BlockSpec((1, half, DEPTH, 128), lambda r, h: (r, h, 0, 0))
    return kernel_call(
        body,
        (lb, query, key, values, d_num, d_den, state, d_own),
        [SMEM, tile, tile, tile, tile, tile, states, states],
        [((3, count, model), BF)],
        [pl.BlockSpec((3, span, width), lambda r, h: (0, r, h))],
        (count // span, model // width),
        scratch=[pltpu.VMEM((span, span), F32)] * 2,
        after=after,
        flops=32 * count * span * model // 4,
    )[0]


def first_norm_grads(d_mixed, w_qkv, tokens, d_middle, gain, after=()):
    parts, count, model = d_mixed.shape
    steps = parts * model // TILE
    per = model // TILE

    def body(d, w, x, dm, g, out, g_gain, g_bias, total):
        j = pl.program_id(0)

        @pl.when(j == 0)
        def _():
            total[...] = dot_nt(d[...], w[...])

        @pl.when(j > 0)
        def _():
            total[...] += dot_nt(d[...], w[...])

        @pl.when(j == steps - 1)
        def _():
            back, g_gain[...], g_bias[...] = norm_grad(total[...], x[...].astype(F32), g[...])
            out[...] = dm[...] + back

    vec = ((1, model), F32)
    return kernel_call(
        body,
        (d_mixed, w_qkv, tokens, d_middle, gain),
        [
            pl.BlockSpec((None, count, TILE), lambda j: (j // per, 0, lax.rem(j, per))),
            pl.BlockSpec((model, TILE), lambda j: (0, j)),
            full((count, model)),
            full((count, model)),
            full((1, model)),
        ],
        [((count, model), F32), vec, vec],
        [full((count, model)), *[full((1, model))] * 2],
        (steps,),
        scratch=[pltpu.VMEM((count, model), F32)],
        after=after,
        flops=2 * count * model * model * parts,
    )


def layer_result(hidden, w_down, middle, down_bias, after=()):
    count, ff = hidden.shape
    model = w_down.shape[1]
    steps = ff // TILE

    def body(h, w, mid, b, out, total):
        j = pl.program_id(0)

        @pl.when(j == 0)
        def _():
            total[...] = mid[...] + b[...] + dot(h[...], w[...])

        @pl.when(j > 0)
        def _():
            total[...] += dot(h[...], w[...])

        @pl.when(j == steps - 1)
        def _():
            out[...] = total[...].astype(BF)

    return kernel_call(
        body,
        (hidden, w_down, middle, down_bias),
        [
            pl.BlockSpec((count, TILE), lambda j: (0, j)),
            pl.BlockSpec((TILE, model), lambda j: (j, 0)),
            full((count, model)),
            full((1, model)),
        ],
        [((count, model), BF)],
        [full((count, model))],
        (steps,),
        scratch=[pltpu.VMEM((count, model), F32)],
        after=after,
        flops=2 * count * model * ff,
    )[0]


def swap(v, pairs):
    return lax.ppermute(v, AXES, pairs)


def states_before(own, doc_end, n_rows, n_seq, later=False):
    me = lax.axis_index("seq")

    def reaches(a, b):
        def at(i):
            return lax.dynamic_index_in_dim(doc_end, i, 1, keepdims=False)

        return (at(a) == at(b)).astype(F32)[:, None, None, None]

    total = own.astype(F32)
    found = jnp.zeros_like(total)
    size = 1
    while size < n_seq:
        pairs = [(r * n_seq + s, r * n_seq + (s ^ size)) for r in range(n_rows) for s in range(n_seq)]
        if 2 * size == n_seq:
            pairs = [p for p in pairs if bool(p[0] % n_seq & size) == later]
        got = swap(total.astype(BF), pairs).astype(F32)
        bit = (me // size) % 2
        group = me // (2 * size) * (2 * size)
        low, mid, high = group, group + size, group + 2 * size
        if later:
            found = found + jnp.where(bit == 0, reaches(me + 1, mid) * got, 0.0)
            same = reaches(low, mid)
            total = jnp.where(bit == 0, total + same * got, got + same * total)
        else:
            found = found + jnp.where(bit == 1, reaches(mid, me) * got, 0.0)
            same = reaches(mid, high)
            total = jnp.where(bit == 0, got + same * total, total + same * got)
        size *= 2
    return found


def stage_pairs(n_rows, n_seq):
    def pairs(bit0, bit1):
        return [(i, i ^ (bit1 if i & 1 else bit0)) for i in range(n_rows * n_seq)]

    return [pairs(2, 4), pairs(8, 8), pairs(4, 2), pairs(16, 16)]


def core_pairs(n):
    return [(i, i ^ 1) for i in range(n)]


def shard_order(device):
    j = jnp.arange(32, dtype=jnp.int32)
    core = device & 1
    first, second = jnp.where(core == 0, 1, 2), jnp.where(core == 0, 2, 1)
    flip = 31 - j
    bit = lambda k: (flip >> k) & 1
    move = bit(4) << first | bit(3) << 3 | bit(2) << second | bit(1) << 4 | bit(0)
    return device ^ move


def halvings(send, keep, stages):
    for k, pairs in enumerate(stages):
        total = keep.astype(F32) + swap(send, pairs).astype(F32)
        if k == len(stages) - 1:
            return total
        half = total.shape[0] // 2
        send, keep = total[:half].astype(BF), total[half:]


def cores_join(total, core, n):
    half = total.shape[0] // 2
    got = swap(total[:half].astype(BF), core_pairs(n)).astype(F32)
    mine = total[half:]
    return jnp.where(core == 0, mine, got), jnp.where(core == 0, got, mine)


def local(
    tokens, bounds, norm1_gain, norm1_bias, w_qkv, w_proj, norm2_gain, norm2_bias,
    w_up, up_bias, w_down, down_bias, cotangent, n_rows, n_seq,
):
    rows, span, model = tokens.shape
    ff = w_up.shape[1]
    count, n = rows * span, n_rows * n_seq
    seq = lax.axis_index("seq")
    device = lax.axis_index("rows") * n_seq + seq
    core = device & 1
    lb = bounds - seq * span
    ends = jnp.arange(n_seq + 1, dtype=jnp.int32) * span - 1
    doc_end = jnp.sum((bounds[:, None, :] <= ends[None, :, None]).astype(jnp.int32), -1)
    x, cot = tokens.reshape(count, model), cotangent.reshape(count, model)
    vec = lambda v: v.reshape(1, -1)
    gain1, bias1, gain2, bias2 = map(vec, (norm1_gain, norm1_bias, norm2_gain, norm2_bias))

    n1, km, v, own = keys_values(lb, x, gain1, bias1, w_qkv, span)
    state = states_before(own, doc_end, n_rows, n_seq)
    qm = queries(n1, w_qkv, after=(own,))
    d_act = active_grads(cot, w_down, after=(qm,))
    numer, denom = attend_inside(lb, qm, km, v, span, after=(d_act,))
    att, rden, middle, n2 = attend_join(lb, state, qm, numer, denom, x, w_proj, gain2, bias2, span)
    hidden, hidden_t, d_pre, g_up_bias = expand(n2, w_up, vec(up_bias), d_act)

    shards = 32
    fast = n == shards and model % (shards * 32) == 0 and ff % (shards * 128) == 0
    if fast:
        stages = stage_pairs(n_rows, n_seq)
        order = shard_order(device)
        place = jnp.zeros((shards,), jnp.int32).at[order].set(jnp.arange(shards, dtype=jnp.int32))
        own_table = jnp.concatenate([order, core[None]])
        other_table = jnp.concatenate([shard_order(device ^ 1), 1 - core[None]])

        def grad_pair(lhs_t, rhs, first, steps, side, after=()):
            per = rhs.shape[-1] // TILE

            def block_of(j, t):
                at = t[shards] * side + first + j
                return (0, at) if rhs.ndim == 2 else (at // per, 0, lax.rem(at, per))

            other = weight_grad(lhs_t, rhs, block_of, steps, other_table, after=after)
            got = swap(other, core_pairs(n))
            return lambda after=(): weight_grad(lhs_t, rhs, block_of, steps, own_table, got, after=after)

        def down_pair(k, per_side, after=()):
            width = model // 2 // per_side
            column = lambda t: t[shards] * per_side + k
            other = down_grad(hidden_t, cot, width, column, other_table, after=after)
            got = swap(other, core_pairs(n))
            return lambda after=(): down_grad(hidden_t, cot, width, column, own_table, got, after=after)

        down1 = down_pair(0, 2)
        down2 = down_pair(1, 2)
        s_d1 = down1()
        s_d2 = down2()
        n2_t = turned(n2, place, shards)
        up1 = grad_pair(n2_t, d_pre, 0, 2, 4)
        up2 = grad_pair(n2_t, d_pre, 2, 2, 4)
        s_u1 = up1()
        s_u2 = up2()
    d_mid, branch, g_gain2, g_bias2, g_down_bias = second_norm_grads(d_pre, w_up, middle, cot, gain2)
    d_num, d_den, d_state = mixer_grads(lb, branch, w_proj, att, rden, qm, span)
    d_own = states_before(d_state, doc_end, n_rows, n_seq, later=True)
    if fast:
        att_t = turned(att, place, shards)
        s_p = grad_pair(att_t, branch, 0, 1, 1)()
        n1_t = turned(n1, place, shards)
    layer_out = layer_result(hidden, w_down, middle, vec(down_bias))
    d_mixed = attend_back(lb, qm, km, v, d_num, d_den, state, d_own, span)
    if fast:
        q1 = grad_pair(n1_t, d_mixed, 0, 2, 3)
        q2 = grad_pair(n1_t, d_mixed, 2, 1, 3)
        s_q1 = q1()
        s_q2 = q2()
    grad_tokens, g_gain1, g_bias1 = first_norm_grads(d_mixed, w_qkv, x, d_mid, gain1)
    small = [g_gain1, g_bias1, g_gain2, g_bias2, g_up_bias, g_down_bias]
    if fast:
        done = [cores_join(halvings(*s, stages), core, n) for s in (s_d1, s_d2, s_u1, s_u2, s_p, s_q1, s_q2)]
        join = lambda *pairs: jnp.concatenate([p[0] for p in pairs] + [p[1] for p in pairs], 1)
        g_down, g_up = join(*done[0:2]), join(*done[2:4])
        g_proj, g_qkv = join(done[4]), join(*done[5:7])
        packed = jnp.concatenate([s.reshape(shards, -1) for s in small], 1)
        packed = jnp.take(packed, order, axis=0).reshape(shards // 2, 2, -1)
        sent = packed[:, 0].reshape(2, 2, 2, 2, -1).transpose(2, 1, 0, 3, 4).reshape(shards // 2, -1)
        total = packed[:, 1] + swap(sent, core_pairs(n))
        for pairs in stages:
            half = total.shape[0] // 2
            total = total[half:] + swap(total[:half], pairs)
        cuts, at = [], 0
        for s in small:
            cuts.append(total[0, at : at + s.shape[1] // shards])
            at += s.shape[1] // shards
        small = cuts
    else:
        scatter = lambda g: lax.psum_scatter(g, AXES, scatter_dimension=0, tiled=True)
        flat = d_mixed.transpose(1, 0, 2).reshape(count, 3 * model)
        g_qkv, g_proj, g_up = (scatter(dot_tn(a, b)) for a, b in ((n1, flat), (att, branch), (n2, d_pre)))
        g_down = scatter(dot_tn(hidden, cot))
        small = [scatter(s.reshape(-1)) for s in small]
    shape = (rows, span, model)
    return (
        layer_out.reshape(shape), grad_tokens.reshape(shape), small[0], small[1], g_qkv, g_proj,
        small[2], small[3], g_up, small[4], g_down, small[5],
    )


def solution(mesh):
    wide, row, whole = P("rows", "seq", None), P(AXES), P()
    in_specs = (wide, P("rows", None), *[whole] * 10, wide)
    out_specs = (wide, wide, *[row] * 10)
    body = functools.partial(local, n_rows=mesh.shape["rows"], n_seq=mesh.shape["seq"])
    return jax.shard_map(body, mesh=mesh, in_specs=in_specs, out_specs=out_specs, check_vma=False)
```

time: 813 us -> 350 us (0.43)
  waiting for transfers between devices: 560 us -> 91.5 us
  Pallas kernels: 0 us -> 170 us
  matrix products: 125 us -> 0 us
  blocking collectives: 57.2 us -> 0 us
  starting transfers between devices: 0.25 us -> 46.8 us
  between operations: 15.2 us -> 1.79 us
  other arithmetic: 30.9 us -> 21.2 us
    reduce_scatter x4 -> x0, waiting for transfers between devices: 555 us -> none  [the longest x1 187 us: local(): lax.psum_scatter(grad_down, ('rows', 'seq'), scatter_dimension=0, tiled=T...]
    pallas_call x0 -> x28, Pallas kernels: none -> 170 us  [the longest x14 108 us: kernel_call(): return run(*args, *after)]
    dot_general x27 -> x0, matrix products: 125 us -> none  [the longest x1 15.6 us: local(): jnp.einsum('rtf,rtd->fd', hidden, cotangent, preferred_element_type=jnp.f...]
    ppermute x0 -> x51, waiting for transfers between devices: none -> 91.5 us  [swap(): return lax.ppermute(v, AXES, pairs)]
    ppermute x0 -> x51, starting transfers between devices: none -> 46.8 us  [swap(): return lax.ppermute(v, AXES, pairs)]
    unnamed x1 -> x0, blocking collectives: 40.5 us -> none
    all_gather x3 -> x0, blocking collectives: 16.7 us -> none  [carried_in(): lax.all_gather(part.astype(kind), axis)]
    select_n x16 -> x9, other arithmetic: 12.2 us -> 0.22 us  [the longest x7 0.13 us: cores_join(): return (jnp.where(core == 0, mine, got), jnp.where(core == 0, got, mine))]
  transfers between devices with their start and end apart: 6 -> 51, of which waited for: 5 -> 20; matrix products, arithmetic and copies ran while one was open for 12% -> 6% of each run, Pallas kernels for 0% -> 34%
where the time goes in v1:
time: 350 us; the launch traced here: 348 us
  Pallas kernels  170 us (49%)
  waiting for transfers between devices  91.5 us (26%)
  starting transfers between devices  46.8 us (13%)
  other arithmetic  21.2 us (6%)
  local copies, waits for them, and re-layouts  16.8 us (5%)
    pallas_call x14, Pallas kernels, kernel_call(): return run(*args, *after)  108 us
    ppermute x51, waiting for transfers between devices, swap(): return lax.ppermute(v, AXES, pairs)  91.5 us
    pallas_call x14, Pallas kernels, kernel_call(): pl.pallas_call(wrapped, grid_spec=spec, **common)(table, *args, *after)  62.4 us
    ppermute x51, starting transfers between devices, swap(): return lax.ppermute(v, AXES, pairs)  46.8 us
    unnamed x82, local copies, waits for them, and re-layouts  11.8 us
  transfers between devices with their start and end apart: 51, of which 20 were waited for; matrix products, arithmetic and copies ran while one was open for 6% of the time, Pallas kernels for 34%

profile of v1, /device:TPU:0, one launch (start us, length us, event | category | flops | bytes accessed | tf_op | source)
XLA Modules:
  0.0 348.1 jit_solution(101213059084718195)
XLA Ops:
  2.7 6.9 %shard_map.220 = (bf16[512,1024]{1,0:T(8,128)(2,1)S(1)}, bf16[512,1024]{1,0:T(8,128)(2,1)S(1)}, bf16[512,1024]{1,0:T(8,128)(2,1)S(1)}, bf16[2,8,80,128]{3,2,1,0:T(8,128)(2,1)S(1)}) custom-call(s32[2,4]{1,0:T(2,128)S(1)} %broadcast_subtract_fusion.refs_0_, bf16[512,1024]{1,0:T(8,128)(2,1)} %bitcast.41, f32[1,1024]{1,0:T(1,128)S(1)} %bitcast.45, ...), custom_call_target="tpu_custom_call" | custom-call | flops 2147483648 | bytes 17113120 | tf_op jit(solution)/shard_map/pallas_call | solution.py:63
  12.1 3.0 shard_map.221.refs_2_.refs_1_.refs_5_
  15.1 11.4 %shard_map.222.refs_4_.refs_3_ = f32[512,4096]{1,0:T(8,128)} custom-call(bf16[512,1024]{1,0:T(8,128)(2,1)S(1)} %bitcast.35, bf16[4096,1024]{1,0:T(8,128)(2,1)} %refs_1_.9, bf16[512,1024]{1,0:T(8,128)(2,1)S(1)} %shard_map.221.refs_2_.refs_1_.refs_5_), custom_call_target="tpu_custom_call" | custom-call | flops 4294967296 | bytes 17825792 | tf_op jit(solution)/shard_map/pallas_call | solution.py:63
  29.8 5.6 %shard_map.223 = (f32[512,1024]{1,0:T(8,128)}, f32[512,1024]{1,0:T(8,128)}) custom-call(s32[2,4]{1,0:T(2,128)S(1)} %broadcast_subtract_fusion.refs_0_, bf16[512,1024]{1,0:T(8,128)(2,1)S(1)} %shard_map.221.refs_2_.refs_1_.refs_5_, bf16[512,1024]{1,0:T(8,128)(2,1)S(1)} %copy-done.15, bf16[512,1024]{1,0:T(8,128)(2,1)S(1)} %copy-done.18, ...), custom_call_target="tpu_custom_call" | custom-call | flops 536870912 | bytes 7340064 | tf_op jit(solution)/shard_map/pallas_call | solution.py:63
  36.6 4.4 %collective-permute-start.1 = (bf16[2,8,80,128]{3,2,1,0:T(8,128)(2,1)S(1)}, bf16[2,8,80,128]{3,2,1,0:T(8,128)(2,1)S(1)}, u32[]{:S(2)}, u32[]{:S(2)}) collective-permute-start(bf16[2,8,80,128]{3,2,1,0:T(8,128)(2,1)S(1)} %fusion.1), channel_id=1, source_target_pairs={{0,2},{1,3},{4,6},{5,7},{8,10},{9,11},{12,14},{13,15},{16,18},{17,... | collective-permute-start | bytes 983048 | tf_op jit(solution)/shard_map/ppermute | solution.py:704
  41.6 7.0 %collective-permute-done.1 = bf16[2,8,80,128]{3,2,1,0:T(8,128)(2,1)S(1)} collective-permute-done((bf16[2,8,80,128]{3,2,1,0:T(8,128)(2,1)S(1)}, bf16[2,8,80,128]{3,2,1,0:T(8,128)(2,1)S(1)}, u32[]{:S(2)}, u32[]{:S(2)}) %collective-permute-start.1) | collective-permute-done | bytes 327712 | tf_op jit(solution)/shard_map/ppermute | solution.py:704
  49.9 7.2 %shard_map.224 = (bf16[512,1024]{1,0:T(8,128)(2,1)S(1)}, f32[512,1024]{1,0:T(8,128)}, f32[512,1024]{1,0:T(8,128)}, bf16[512,1024]{1,0:T(8,128)(2,1)S(1)}) custom-call(s32[2,4]{1,0:T(2,128)S(1)} %broadcast_subtract_fusion.refs_0_, f32[2,8,80,128]{3,2,1,0:T(8,128)S(1)} %fusion.5.refs_1_.refs_6_, bf16[512,1024]{1,0:T(8,128)(2,1)S(1)} %shard_map.221.refs_2_.refs_1_.refs_5_, ...), custom_call_target="tpu_custom_call" | custom-call | flops 1610612736 | bytes 15343648 | tf_op jit(solution)/shard_map/pallas_call | solution.py:63
  57.1 17.7 %shard_map.225 = (bf16[512,4096]{1,0:T(8,128)(2,1)}, bf16[4096,512]{1,0:T(8,128)(2,1)}, bf16[512,4096]{1,0:T(8,128)(2,1)}, f32[1,4096]{1,0:T(1,128)S(1)}) custom-call(bf16[512,1024]{1,0:T(8,128)(2,1)S(1)} %get-tuple-element.57.refs_0_.refs_1_, bf16[1024,4096]{1,0:T(8,128)(2,1)} %refs_1_.10, f32[1,4096]{1,0:T(1,128)S(1)} %bitcast.44, ...), custom_call_target="tpu_custom_call" | custom-call | flops 4294967296 | bytes 30441472 | tf_op jit(solution)/shard_map/pallas_call | solution.py:63
  74.9 13.3 %shard_map.227 = (f32[512,1024]{1,0:T(8,128)}, bf16[512,1024]{1,0:T(8,128)(2,1)S(1)}, f32[1,1024]{1,0:T(1,128)S(1)}, f32[1,1024]{1,0:T(1,128)S(1)}, f32[1,1024]{1,0:T(1,128)S(1)}) custom-call(bf16[512,4096]{1,0:T(8,128)(2,1)} %get-tuple-element.60.refs_0_.refs_2_, bf16[1024,4096]{1,0:T(8,128)(2,1)} %refs_1_.10, f32[512,1024]{1,0:T(8,128)} %get-tuple-element.59.refs_2_, ...), custom_call_target="tpu_custom_call" | custom-call | flops 4294967296 | bytes 18890752 | tf_op jit(solution)/shard_map/pallas_call | solution.py:63
  88.2 6.2 %shard_map.228 = (bf16[512,1024]{1,0:T(8,128)(2,1)S(1)}, f32[512,1024]{1,0:T(8,128)}, bf16[2,8,80,128]{3,2,1,0:T(8,128)(2,1)S(1)}) custom-call(s32[2,4]{1,0:T(2,128)S(1)} %broadcast_subtract_fusion.refs_0_, bf16[512,1024]{1,0:T(8,128)(2,1)S(1)} %get-tuple-element.61.refs_1_.refs_2_, bf16[1024,1024]{1,0:T(8,128)(2,1)} %refs_2_.1, ...), custom_call_target="tpu_custom_call" | custom-call | flops 1610612736 | bytes 10813472 | tf_op jit(solution)/shard_map/pallas_call | solution.py:63
  98.5 2.2 shard_map.237
  103.1 2.0 fusion.3
  106.4 7.7 %shard_map.244 = bf16[4096,256]{1,0:T(8,128)(2,1)} custom-call(s32[33]{0:T(128)S(1)} %pad_add_fusion.1.refs_0_, bf16[4096,512]{1,0:T(8,128)(2,1)} %get-tuple-element.85.refs_1_.refs_2_.refs_3_.refs_4_, bf16[4096,512]{1,0:T(8,128)(2,1)} %get-tuple-element.85.refs_1_.refs_2_.refs_3_.refs_4_, ...), custom_call_target="tpu_custom_call" | custom-call | flops 1073741824 | bytes 19922944 | tf_op jit(solution)/shard_map/pallas_call | solution.py:67
  115.1 7.7 %shard_map.246 = bf16[4096,256]{1,0:T(8,128)(2,1)} custom-call(s32[33]{0:T(128)S(1)} %pad_add_fusion.1.refs_0_, bf16[4096,512]{1,0:T(8,128)(2,1)} %get-tuple-element.85.refs_1_.refs_2_.refs_3_.refs_4_, bf16[4096,512]{1,0:T(8,128)(2,1)} %get-tuple-element.85.refs_1_.refs_2_.refs_3_.refs_4_, ...), custom_call_target="tpu_custom_call" | custom-call | flops 1073741824 | bytes 19922944 | tf_op jit(solution)/shard_map/pallas_call | solution.py:67
  126.6 3.2 shard_map.240
  131.2 3.5 shard_map.242
  137.2 12.5 %shard_map.229.refs_0_.refs_2_ = bf16[3,512,1024]{2,1,0:T(8,128)(2,1)} custom-call(s32[2,4]{1,0:T(2,128)S(1)} %broadcast_subtract_fusion.refs_0_, bf16[512,1024]{1,0:T(8,128)(2,1)S(1)} %copy-done.1, bf16[512,1024]{1,0:T(8,128)(2,1)S(1)} %copy-done.16, bf16[512,1024]{1,0:T(8,128)(2,1)} %copy-done.17, bf16[512,1024]{1,0:T(8,128)(2,1)} %copy-done.26, ...), custom_call_target="tpu_custom_call" | custom-call | flops 1073741824 | bytes 10747936 | tf_op jit(solution)/shard_map/pallas_call | solution.py:63
  149.8 3.4 shard_map.238
  153.2 2.6 collective-permute-start.22
  155.8 10.4 %shard_map.230 = (f32[512,1024]{1,0:T(8,128)}, f32[1,1024]{1,0:T(1,128)S(1)}, f32[1,1024]{1,0:T(1,128)S(1)}) custom-call(bf16[3,512,1024]{2,1,0:T(8,128)(2,1)} %shard_map.229.refs_0_.refs_2_, bf16[1024,3072]{1,0:T(8,128)(2,1)} %refs_1_.11, bf16[512,1024]{1,0:T(8,128)(2,1)S(1)} %bitcast.43, f32[512,1024]{1,0:T(8,128)S(1)} %copy-done.23, f32[1,1024]{1,0:T(1,128)S(1)} %bitcast.46), custom_call_target="tpu_custom_call" | custom-call | flops 3221225472 | bytes 14692352 | tf_op jit(solution)/shard_map/pallas_call | solution.py:63
  168.7 2.3 shard_map.234
  175.4 10.8 %shard_map.226 = bf16[512,1024]{1,0:T(8,128)(2,1)} custom-call(bf16[512,4096]{1,0:T(8,128)(2,1)} %get-tuple-element.58.refs_0_, bf16[4096,1024]{1,0:T(8,128)(2,1)} %refs_1_.9, f32[512,1024]{1,0:T(8,128)S(1)} %copy-done.35, f32[1,1024]{1,0:T(1,128)S(1)} %bitcast.52), custom_call_target="tpu_custom_call" | custom-call | flops 4294967296 | bytes 15732736 | tf_op jit(solution)/shard_map/pallas_call | solution.py:63
  187.0 3.1 collective-permute-done.6
  192.2 2.3 shard_map.235
  196.2 2.7 collective-permute-start.25
  198.9 3.2 collective-permute-done.25
  202.0 2.0 collective-permute-start.8
  204.4 2.1 collective-permute-done.8
  206.6 3.2 shard_map.232
  209.8 5.4 %collective-permute-done.17 = bf16[256,512]{1,0:T(8,128)(2,1)S(1)} collective-permute-done((bf16[256,512]{1,0:T(8,128)(2,1)S(1)}, bf16[256,512]{1,0:T(8,128)(2,1)S(1)}, u32[]{:S(2)}, u32[]{:S(2)}) %collective-permute-start.17) | collective-permute-done | bytes 262176 | tf_op jit(solution)/shard_map/ppermute | solution.py:704
  218.7 8.1 %shard_map.245 = (bf16[2048,256]{1,0:T(8,128)(2,1)}, bf16[2048,256]{1,0:T(8,128)(2,1)S(1)}) custom-call(s32[33]{0:T(128)S(1)} %pad_add_fusion.refs_0_, bf16[4096,512]{1,0:T(8,128)(2,1)} %get-tuple-element.85.refs_1_.refs_2_.refs_3_.refs_4_, bf16[4096,512]{1,0:T(8,128)(2,1)} %get-tuple-element.85.refs_1_.refs_2_.refs_3_.refs_4_, ...), custom_call_target="tpu_custom_call" | custom-call | flops 1073741824 | bytes 22020096 | tf_op jit(solution)/shard_map/pallas_call | solution.py:67
  227.1 8.1 %shard_map.247 = (bf16[2048,256]{1,0:T(8,128)(2,1)}, bf16[2048,256]{1,0:T(8,128)(2,1)S(1)}) custom-call(s32[33]{0:T(128)S(1)} %pad_add_fusion.refs_0_, bf16[4096,512]{1,0:T(8,128)(2,1)} %get-tuple-element.85.refs_1_.refs_2_.refs_3_.refs_4_, bf16[4096,512]{1,0:T(8,128)(2,1)} %get-tuple-element.85.refs_1_.refs_2_.refs_3_.refs_4_, ...), custom_call_target="tpu_custom_call" | custom-call | flops 1073741824 | bytes 22020096 | tf_op jit(solution)/shard_map/pallas_call | solution.py:67
  237.2 2.0 collective-permute-start.19
  239.3 3.5 %shard_map.241 = (bf16[512,1024]{1,0:T(8,128)(2,1)S(1)}, bf16[512,1024]{1,0:T(8,128)(2,1)S(1)}) custom-call(s32[33]{0:T(128)S(1)} %pad_add_fusion.refs_0_, bf16[1024,512]{1,0:T(8,128)(2,1)S(1)} %shard_map.239.refs_1_, bf16[512,4096]{1,0:T(8,128)(2,1)} %get-tuple-element.60.refs_0_.refs_2_, bf16[1024,1024]{1,0:T(8,128)(2,1)} %collective-permute-done.27.refs_3_), custom_call_target="tpu_custom_call" | custom-call | flops 1073741824 | bytes 9437184 | tf_op jit(solution)/shard_map/pallas_call | solution.py:67
  243.6 3.5 %shard_map.243 = (bf16[512,1024]{1,0:T(8,128)(2,1)S(1)}, bf16[512,1024]{1,0:T(8,128)(2,1)S(1)}) custom-call(s32[33]{0:T(128)S(1)} %pad_add_fusion.refs_0_, bf16[1024,512]{1,0:T(8,128)(2,1)S(1)} %shard_map.239.refs_1_, bf16[512,4096]{1,0:T(8,128)(2,1)} %get-tuple-element.60.refs_0_.refs_2_, bf16[1024,1024]{1,0:T(8,128)(2,1)} %collective-permute-done.33.refs_3_), custom_call_target="tpu_custom_call" | custom-call | flops 1073741824 | bytes 9437184 | tf_op jit(solution)/shard_map/pallas_call | solution.py:67
  248.7 3.6 %shard_map.233 = (bf16[512,1024]{1,0:T(8,128)(2,1)S(1)}, bf16[512,1024]{1,0:T(8,128)(2,1)S(1)}) custom-call(s32[33]{0:T(128)S(1)} %pad_add_fusion.refs_0_, bf16[1024,512]{1,0:T(8,128)(2,1)S(1)} %shard_map.231.refs_1_, bf16[3,512,1024]{2,1,0:T(8,128)(2,1)} %shard_map.229.refs_0_.refs_2_, bf16[1024,1024]{1,0:T(8,128)(2,1)} %collective-permute-done.9.refs_3_), custom_call_target="tpu_custom_call" | custom-call | flops 1073741824 | bytes 8388608 | tf_op jit(solution)/shard_map/pallas_call | solution.py:67
  258.1 6.3 %collective-permute-done.28 = bf16[512,1024]{1,0:T(8,128)(2,1)S(1)} collective-permute-done((bf16[512,1024]{1,0:T(8,128)(2,1)S(1)}, bf16[512,1024]{1,0:T(8,128)(2,1)S(1)}, u32[]{:S(2)}, u32[]{:S(2)}) %collective-permute-start.28) | collective-permute-done | bytes 1048608 | tf_op jit(solution)/shard_map/ppermute | solution.py:704
  265.2 10.4 %collective-permute-done.34 = bf16[512,1024]{1,0:T(8,128)(2,1)S(1)} collective-permute-done((bf16[512,1024]{1,0:T(8,128)(2,1)S(1)}, bf16[512,1024]{1,0:T(8,128)(2,1)S(1)}, u32[]{:S(2)}, u32[]{:S(2)}) %collective-permute-start.34) | collective-permute-done | bytes 1048608 | tf_op jit(solution)/shard_map/ppermute | solution.py:704
  277.2 3.4 collective-permute-done.47
  282.3 9.5 %collective-permute-done.29 = bf16[256,1024]{1,0:T(8,128)(2,1)S(1)} collective-permute-done((bf16[256,1024]{1,0:T(8,128)(2,1)S(1)}, bf16[256,1024]{1,0:T(8,128)(2,1)S(1)}, u32[]{:S(2)}, u32[]{:S(2)}) %collective-permute-start.29) | collective-permute-done | bytes 524320 | tf_op jit(solution)/shard_map/ppermute | solution.py:704
  293.6 8.4 %collective-permute-done.35 = bf16[256,1024]{1,0:T(8,128)(2,1)S(1)} collective-permute-done((bf16[256,1024]{1,0:T(8,128)(2,1)S(1)}, bf16[256,1024]{1,0:T(8,128)(2,1)S(1)}, u32[]{:S(2)}, u32[]{:S(2)}) %collective-permute-start.35) | collective-permute-done | bytes 524320 | tf_op jit(solution)/shard_map/ppermute | solution.py:704
  304.7 2.5 collective-permute-start.43
  308.0 2.5 collective-permute-start.31
  311.1 8.7 %collective-permute-done.43 = bf16[256,256]{1,0:T(8,128)(2,1)S(1)} collective-permute-done((bf16[256,256]{1,0:T(8,128)(2,1)S(1)}, bf16[256,256]{1,0:T(8,128)(2,1)S(1)}, u32[]{:S(2)}, u32[]{:S(2)}) %collective-permute-start.43) | collective-permute-done | bytes 131104 | tf_op jit(solution)/shard_map/ppermute | solution.py:704
  320.0 2.7 collective-permute-done.49
  324.9 4.5 %collective-permute-done.37 = bf16[64,1024]{1,0:T(8,128)(2,1)S(1)} collective-permute-done((bf16[64,1024]{1,0:T(8,128)(2,1)S(1)}, bf16[64,1024]{1,0:T(8,128)(2,1)S(1)}, u32[]{:S(2)}, u32[]{:S(2)}) %collective-permute-start.37) | collective-permute-done | bytes 131104 | tf_op jit(solution)/shard_map/ppermute | solution.py:704
  333.1 4.4 %collective-permute-done.12 = bf16[128,1024]{1,0:T(8,128)(2,1)S(1)} collective-permute-done((bf16[128,1024]{1,0:T(8,128)(2,1)S(1)}, bf16[128,1024]{1,0:T(8,128)(2,1)S(1)}, u32[]{:S(2)}, u32[]{:S(2)}) %collective-permute-start.12) | collective-permute-done | bytes 262176 | tf_op jit(solution)/shard_map/ppermute | solution.py:704
  337.8 8.1 %collective-permute-done.13 = bf16[64,1024]{1,0:T(8,128)(2,1)S(1)} collective-permute-done((bf16[64,1024]{1,0:T(8,128)(2,1)S(1)}, bf16[64,1024]{1,0:T(8,128)(2,1)S(1)}, u32[]{:S(2)}, u32[]{:S(2)}) %collective-permute-start.13) | collective-permute-done | bytes 131104 | tf_op jit(solution)/shard_map/ppermute | solution.py:704
  (278 shorter events, 70.9 us)
Async XLA Ops:
  11.6 23.8 %collective-permute-start = (bf16[2,8,80,128]{3,2,1,0:T(8,128)(2,1)S(1)}, bf16[2,8,80,128]{3,2,1,0:T(8,128)(2,1)}, u32[]{:S(2)}, u32[]{:S(2)}) collective-permute-start(bf16[2,8,80,128]{3,2,1,0:T(8,128)(2,1)S(1)} %get-tuple-element.51.refs_2_), channel_id=1, source_target_pairs={{0,1},{1,0},{2,3},{3,2},{4,5},{5,4},{6,7},{7,6},{8,9},{9,8},{10,11... | collective-permute-start | bytes 983048 | tf_op jit(solution)/shard_map/ppermute | solution.py:704
  36.6 12.0 %collective-permute-start.1 = (bf16[2,8,80,128]{3,2,1,0:T(8,128)(2,1)S(1)}, bf16[2,8,80,128]{3,2,1,0:T(8,128)(2,1)S(1)}, u32[]{:S(2)}, u32[]{:S(2)}) collective-permute-start(bf16[2,8,80,128]{3,2,1,0:T(8,128)(2,1)S(1)} %fusion.1), channel_id=1, source_target_pairs={{0,2},{1,3},{4,6},{5,7},{8,10},{9,11},{12,14},{13,15},{16,18},{17,... | collective-permute-start | bytes 983048 | tf_op jit(solution)/shard_map/ppermute | solution.py:704
  95.4 7.7 %collective-permute-start.2 = (bf16[2,8,80,128]{3,2,1,0:T(8,128)(2,1)S(1)}, bf16[2,8,80,128]{3,2,1,0:T(8,128)(2,1)}, u32[]{:S(2)}, u32[]{:S(2)}) collective-permute-start(bf16[2,8,80,128]{3,2,1,0:T(8,128)(2,1)S(1)} %get-tuple-element.66), channel_id=1, source_target_pairs={{0,1},{1,0},{2,3},{3,2},{4,5},{5,4},{6,7},{7,6},{8,9},{9,8},{10,11... | collective-permute-start | bytes 983048 | tf_op jit(solution)/shard_map/ppermute | solution.py:704
  101.6 48.1 %collective-permute-start.21 = (bf16[1024,512]{1,0:T(8,128)(2,1)}, bf16[1024,512]{1,0:T(8,128)(2,1)}, u32[]{:S(2)}, u32[]{:S(2)}) collective-permute-start(bf16[1024,512]{1,0:T(8,128)(2,1)} %shard_map.237), channel_id=1, source_target_pairs={{0,1},{1,0},{2,3},{3,2},{4,5},{5,4},{6,7},{7,6},{8,9},{9,8},{10,11... | collective-permute-start | bytes 3145736 | tf_op jit(solution)/shard_map/ppermute | solution.py:704
  105.1 30.9 %collective-permute-start.3 = (bf16[2,8,80,128]{3,2,1,0:T(8,128)(2,1)}, bf16[2,8,80,128]{3,2,1,0:T(8,128)(2,1)S(1)}, u32[]{:S(2)}, u32[]{:S(2)}) collective-permute-start(bf16[2,8,80,128]{3,2,1,0:T(8,128)(2,1)} %fusion.3), channel_id=1, source_target_pairs={{2,0},{3,1},{6,4},{7,5},{10,8},{11,9},{14,12},{15,13},{18,16},{19,... | collective-permute-start | bytes 983048 | tf_op jit(solution)/shard_map/ppermute | solution.py:704
  115.0 102.1 %collective-permute-start.39 = (bf16[4096,256]{1,0:T(8,128)(2,1)}, bf16[4096,256]{1,0:T(8,128)(2,1)}, u32[]{:S(2)}, u32[]{:S(2)}) collective-permute-start(bf16[4096,256]{1,0:T(8,128)(2,1)} %shard_map.244), channel_id=1, source_target_pairs={{0,1},{1,0},{2,3},{3,2},{4,5},{5,4},{6,7},{7,6},{8,9},{9,8},{10,11... | collective-permute-start | bytes 6291464 | tf_op jit(solution)/shard_map/ppermute | solution.py:704
  122.8 104.1 %collective-permute-start.45 = (bf16[4096,256]{1,0:T(8,128)(2,1)}, bf16[4096,256]{1,0:T(8,128)(2,1)}, u32[]{:S(2)}, u32[]{:S(2)}) collective-permute-start(bf16[4096,256]{1,0:T(8,128)(2,1)} %shard_map.246), channel_id=1, source_target_pairs={{0,1},{1,0},{2,3},{3,2},{4,5},{5,4},{6,7},{7,6},{8,9},{9,8},{10,11... | collective-permute-start | bytes 6291464 | tf_op jit(solution)/shard_map/ppermute | solution.py:704
  153.2 19.3 %collective-permute-start.22 = (bf16[512,512]{1,0:T(8,128)(2,1)}, bf16[512,512]{1,0:T(8,128)(2,1)}, u32[]{:S(2)}, u32[]{:S(2)}) collective-permute-start(bf16[512,512]{1,0:T(8,128)(2,1)} %get-tuple-element.80), channel_id=1, source_target_pairs={{0,2},{1,5},{2,0},{3,7},{4,6},{5,1},{6,4},{7,3},{8,10},{9,13},{10,... | collective-permute-start | bytes 1572872 | tf_op jit(solution)/shard_map/ppermute | solution.py:704
  168.6 3.0 collective-permute-start.4
  171.0 19.8 %collective-permute-start.15 = (bf16[1024,512]{1,0:T(8,128)(2,1)S(1)}, bf16[1024,512]{1,0:T(8,128)(2,1)S(1)}, u32[]{:S(2)}, u32[]{:S(2)}) collective-permute-start(bf16[1024,512]{1,0:T(8,128)(2,1)S(1)} %shard_map.234), channel_id=1, source_target_pairs={{0,1},{1,0},{2,3},{3,2},{4,5},{5,4},{6,7},{7,6},{8,9},{9,8},{10,11... | collective-permute-start | bytes 3145736 | tf_op jit(solution)/shard_map/ppermute | solution.py:704
  171.6 14.5 %collective-permute-start.5 = (f32[8,288]{1,0:T(8,128)S(1)}, f32[8,288]{1,0:T(8,128)S(1)}, u32[]{:S(2)}, u32[]{:S(2)}) collective-permute-start(f32[8,288]{1,0:T(8,128)S(1)} %slice.321), channel_id=1, source_target_pairs={{0,2},{1,5},{2,0},{3,7},{4,6},{5,1},{6,4},{7,3},{8,10},{9,13},{10,... | collective-permute-start | bytes 27656 | tf_op jit(solution)/shard_map/ppermute | solution.py:704
  173.7 12.7 %collective-permute-start.23 = (bf16[256,512]{1,0:T(8,128)(2,1)S(1)}, bf16[256,512]{1,0:T(8,128)(2,1)S(1)}, u32[]{:S(2)}, u32[]{:S(2)}) collective-permute-start(bf16[256,512]{1,0:T(8,128)(2,1)S(1)} %slice.475), channel_id=1, source_target_pairs={{0,8},{1,9},{2,10},{3,11},{4,12},{5,13},{6,14},{7,15},{8,0},{9,1},... | collective-permute-start | bytes 786440 | tf_op jit(solution)/shard_map/ppermute | solution.py:704
  186.1 51.1 %collective-permute-start.27 = (bf16[1024,1024]{1,0:T(8,128)(2,1)S(1)}, bf16[1024,1024]{1,0:T(8,128)(2,1)}, u32[]{:S(2)}, u32[]{:S(2)}) collective-permute-start(bf16[1024,1024]{1,0:T(8,128)(2,1)S(1)} %copy-done.22), channel_id=1, source_target_pairs={{0,1},{1,0},{2,3},{3,2},{4,5},{5,4},{6,7},{7,6},{8,9},{9,8},{10,11... | collective-permute-start | bytes 6291464 | tf_op jit(solution)/shard_map/ppermute | solution.py:704
  186.4 3.7 %collective-permute-start.6 = (f32[4,288]{1,0:T(4,128)S(1)}, f32[4,288]{1,0:T(4,128)S(1)}, u32[]{:S(2)}, u32[]{:S(2)}) collective-permute-start(f32[4,288]{1,0:T(4,128)S(1)} %slice.323), channel_id=1, source_target_pairs={{0,8},{1,9},{2,10},{3,11},{4,12},{5,13},{6,14},{7,15},{8,0},{9,1},... | collective-permute-start | bytes 13832 | tf_op jit(solution)/shard_map/ppermute | solution.py:704
  190.1 5.0 %collective-permute-start.24 = (bf16[128,512]{1,0:T(8,128)(2,1)S(1)}, bf16[128,512]{1,0:T(8,128)(2,1)S(1)}, u32[]{:S(2)}, u32[]{:S(2)}) collective-permute-start(bf16[128,512]{1,0:T(8,128)(2,1)S(1)} %slice.482), channel_id=1, source_target_pairs={{0,4},{1,3},{2,6},{3,1},{4,0},{5,7},{6,2},{7,5},{8,12},{9,11},{10,... | collective-permute-start | bytes 393224 | tf_op jit(solution)/shard_map/ppermute | solution.py:704
  190.9 5.3 %collective-permute-start.7 = (f32[2,288]{1,0:T(2,128)S(1)}, f32[2,288]{1,0:T(2,128)S(1)}, u32[]{:S(2)}, u32[]{:S(2)}) collective-permute-start(f32[2,288]{1,0:T(2,128)S(1)} %slice.325), channel_id=1, source_target_pairs={{0,4},{1,3},{2,6},{3,1},{4,0},{5,7},{6,2},{7,5},{8,12},{9,11},{10,... | collective-permute-start | bytes 6920 | tf_op jit(solution)/shard_map/ppermute | solution.py:704
  195.1 9.2 %collective-permute-start.16 = (bf16[512,512]{1,0:T(8,128)(2,1)S(1)}, bf16[512,512]{1,0:T(8,128)(2,1)S(1)}, u32[]{:S(2)}, u32[]{:S(2)}) collective-permute-start(bf16[512,512]{1,0:T(8,128)(2,1)S(1)} %get-tuple-element.78), channel_id=1, source_target_pairs={{0,2},{1,5},{2,0},{3,7},{4,6},{5,1},{6,4},{7,3},{8,10},{9,13},{10,... | collective-permute-start | bytes 1572872 | tf_op jit(solution)/shard_map/ppermute | solution.py:704
  196.2 5.8 %collective-permute-start.25 = (bf16[64,512]{1,0:T(8,128)(2,1)S(1)}, bf16[64,512]{1,0:T(8,128)(2,1)S(1)}, u32[]{:S(2)}, u32[]{:S(2)}) collective-permute-start(bf16[64,512]{1,0:T(8,128)(2,1)S(1)} %slice.489), channel_id=1, source_target_pairs={{0,16},{1,17},{2,18},{3,19},{4,20},{5,21},{6,22},{7,23},{8,24},{9,... | collective-permute-start | bytes 196616 | tf_op jit(solution)/shard_map/ppermute | solution.py:704
  202.0 4.5 %collective-permute-start.8 = (f32[1,288]{1,0:T(1,128)S(1)}, f32[1,288]{1,0:T(1,128)S(1)}, u32[]{:S(2)}, u32[]{:S(2)}) collective-permute-start(f32[1,288]{1,0:T(1,128)S(1)} %slice.327), channel_id=1, source_target_pairs={{0,16},{1,17},{2,18},{3,19},{4,20},{5,21},{6,22},{7,23},{8,24},{9,... | collective-permute-start | bytes 3464 | tf_op jit(solution)/shard_map/ppermute | solution.py:704
  206.5 37.0 %collective-permute-start.33 = (bf16[1024,1024]{1,0:T(8,128)(2,1)S(1)}, bf16[1024,1024]{1,0:T(8,128)(2,1)}, u32[]{:S(2)}, u32[]{:S(2)}) collective-permute-start(bf16[1024,1024]{1,0:T(8,128)(2,1)S(1)} %copy-done.20), channel_id=1, source_target_pairs={{0,1},{1,0},{2,3},{3,2},{4,5},{5,4},{6,7},{7,6},{8,9},{9,8},{10,11... | collective-permute-start | bytes 6291464 | tf_op jit(solution)/shard_map/ppermute | solution.py:704
  206.5 8.7 %collective-permute-start.17 = (bf16[256,512]{1,0:T(8,128)(2,1)S(1)}, bf16[256,512]{1,0:T(8,128)(2,1)S(1)}, u32[]{:S(2)}, u32[]{:S(2)}) collective-permute-start(bf16[256,512]{1,0:T(8,128)(2,1)S(1)} %slice.476), channel_id=1, source_target_pairs={{0,8},{1,9},{2,10},{3,11},{4,12},{5,13},{6,14},{7,15},{8,0},{9,1},... | collective-permute-start | bytes 786440 | tf_op jit(solution)/shard_map/ppermute | solution.py:704
  215.2 33.5 %collective-permute-start.9 = (bf16[1024,1024]{1,0:T(8,128)(2,1)S(1)}, bf16[1024,1024]{1,0:T(8,128)(2,1)}, u32[]{:S(2)}, u32[]{:S(2)}) collective-permute-start(bf16[1024,1024]{1,0:T(8,128)(2,1)S(1)} %shard_map.232), channel_id=1, source_target_pairs={{0,1},{1,0},{2,3},{3,2},{4,5},{5,4},{6,7},{7,6},{8,9},{9,8},{10,11... | collective-permute-start | bytes 6291464 | tf_op jit(solution)/shard_map/ppermute | solution.py:704
  217.1 18.1 %collective-permute-start.18 = (bf16[128,512]{1,0:T(8,128)(2,1)S(1)}, bf16[128,512]{1,0:T(8,128)(2,1)S(1)}, u32[]{:S(2)}, u32[]{:S(2)}) collective-permute-start(bf16[128,512]{1,0:T(8,128)(2,1)S(1)} %slice.483), channel_id=1, source_target_pairs={{0,4},{1,3},{2,6},{3,1},{4,0},{5,7},{6,2},{7,5},{8,12},{9,11},{10,... | collective-permute-start | bytes 393224 | tf_op jit(solution)/shard_map/ppermute | solution.py:704
  226.9 26.1 %collective-permute-start.40 = (bf16[2048,256]{1,0:T(8,128)(2,1)}, bf16[2048,256]{1,0:T(8,128)(2,1)}, u32[]{:S(2)}, u32[]{:S(2)}) collective-permute-start(bf16[2048,256]{1,0:T(8,128)(2,1)} %get-tuple-element.87), channel_id=1, source_target_pairs={{0,2},{1,5},{2,0},{3,7},{4,6},{5,1},{6,4},{7,3},{8,10},{9,13},{10,... | collective-permute-start | bytes 3145736 | tf_op jit(solution)/shard_map/ppermute | solution.py:704
  235.2 19.4 %collective-permute-start.46 = (bf16[2048,256]{1,0:T(8,128)(2,1)}, bf16[2048,256]{1,0:T(8,128)(2,1)}, u32[]{:S(2)}, u32[]{:S(2)}) collective-permute-start(bf16[2048,256]{1,0:T(8,128)(2,1)} %get-tuple-element.89), channel_id=1, source_target_pairs={{0,2},{1,5},{2,0},{3,7},{4,6},{5,1},{6,4},{7,3},{8,10},{9,13},{10,... | collective-permute-start | bytes 3145736 | tf_op jit(solution)/shard_map/ppermute | solution.py:704
  237.2 5.6 %collective-permute-start.19 = (bf16[64,512]{1,0:T(8,128)(2,1)S(1)}, bf16[64,512]{1,0:T(8,128)(2,1)S(1)}, u32[]{:S(2)}, u32[]{:S(2)}) collective-permute-start(bf16[64,512]{1,0:T(8,128)(2,1)S(1)} %slice.490), channel_id=1, source_target_pairs={{0,16},{1,17},{2,18},{3,19},{4,20},{5,21},{6,22},{7,23},{8,24},{9,... | collective-permute-start | bytes 196616 | tf_op jit(solution)/shard_map/ppermute | solution.py:704
  242.9 21.5 %collective-permute-start.28 = (bf16[512,1024]{1,0:T(8,128)(2,1)S(1)}, bf16[512,1024]{1,0:T(8,128)(2,1)S(1)}, u32[]{:S(2)}, u32[]{:S(2)}) collective-permute-start(bf16[512,1024]{1,0:T(8,128)(2,1)S(1)} %get-tuple-element.82), channel_id=1, source_target_pairs={{0,2},{1,5},{2,0},{3,7},{4,6},{5,1},{6,4},{7,3},{8,10},{9,13},{10,... | collective-permute-start | bytes 3145736 | tf_op jit(solution)/shard_map/ppermute | solution.py:704
  243.5 3.6 %collective-permute-start.20 = (bf16[32,512]{1,0:T(8,128)(2,1)S(1)}, bf16[32,512]{1,0:T(8,128)(2,1)S(1)}, u32[]{:S(2)}, u32[]{:S(2)}) collective-permute-start(bf16[32,512]{1,0:T(8,128)(2,1)S(1)} %slice.493), channel_id=1, source_target_pairs={{0,1},{1,0},{2,3},{3,2},{4,5},{5,4},{6,7},{7,6},{8,9},{9,8},{10,11... | collective-permute-start | bytes 98312 | tf_op jit(solution)/shard_map/ppermute | solution.py:704
  247.2 28.5 %collective-permute-start.34 = (bf16[512,1024]{1,0:T(8,128)(2,1)S(1)}, bf16[512,1024]{1,0:T(8,128)(2,1)S(1)}, u32[]{:S(2)}, u32[]{:S(2)}) collective-permute-start(bf16[512,1024]{1,0:T(8,128)(2,1)S(1)} %get-tuple-element.84), channel_id=1, source_target_pairs={{0,2},{1,5},{2,0},{3,7},{4,6},{5,1},{6,4},{7,3},{8,10},{9,13},{10,... | collective-permute-start | bytes 3145736 | tf_op jit(solution)/shard_map/ppermute | solution.py:704
  252.3 51.5 %collective-permute-start.10 = (bf16[512,1024]{1,0:T(8,128)(2,1)S(1)}, bf16[512,1024]{1,0:T(8,128)(2,1)S(1)}, u32[]{:S(2)}, u32[]{:S(2)}) collective-permute-start(bf16[512,1024]{1,0:T(8,128)(2,1)S(1)} %get-tuple-element.76), channel_id=1, source_target_pairs={{0,2},{1,5},{2,0},{3,7},{4,6},{5,1},{6,4},{7,3},{8,10},{9,13},{10,... | collective-permute-start | bytes 3145736 | tf_op jit(solution)/shard_map/ppermute | solution.py:704
  254.5 22.0 %collective-permute-start.41 = (bf16[1024,256]{1,0:T(8,128)(2,1)S(1)}, bf16[1024,256]{1,0:T(8,128)(2,1)S(1)}, u32[]{:S(2)}, u32[]{:S(2)}) collective-permute-start(bf16[1024,256]{1,0:T(8,128)(2,1)S(1)} %slice.467), channel_id=1, source_target_pairs={{0,8},{1,9},{2,10},{3,11},{4,12},{5,13},{6,14},{7,15},{8,0},{9,1},... | collective-permute-start | bytes 1572872 | tf_op jit(solution)/shard_map/ppermute | solution.py:704
  256.2 24.4 %collective-permute-start.47 = (bf16[1024,256]{1,0:T(8,128)(2,1)S(1)}, bf16[1024,256]{1,0:T(8,128)(2,1)S(1)}, u32[]{:S(2)}, u32[]{:S(2)}) collective-permute-start(bf16[1024,256]{1,0:T(8,128)(2,1)S(1)} %slice.466), channel_id=1, source_target_pairs={{0,8},{1,9},{2,10},{3,11},{4,12},{5,13},{6,14},{7,15},{8,0},{9,1},... | collective-permute-start | bytes 1572872 | tf_op jit(solution)/shard_map/ppermute | solution.py:704
  264.9 26.9 %collective-permute-start.29 = (bf16[256,1024]{1,0:T(8,128)(2,1)S(1)}, bf16[256,1024]{1,0:T(8,128)(2,1)S(1)}, u32[]{:S(2)}, u32[]{:S(2)}) collective-permute-start(bf16[256,1024]{1,0:T(8,128)(2,1)S(1)} %slice.469), channel_id=1, source_target_pairs={{0,8},{1,9},{2,10},{3,11},{4,12},{5,13},{6,14},{7,15},{8,0},{9,1},... | collective-permute-start | bytes 1572872 | tf_op jit(solution)/shard_map/ppermute | solution.py:704
  276.1 25.9 %collective-permute-start.35 = (bf16[256,1024]{1,0:T(8,128)(2,1)S(1)}, bf16[256,1024]{1,0:T(8,128)(2,1)S(1)}, u32[]{:S(2)}, u32[]{:S(2)}) collective-permute-start(bf16[256,1024]{1,0:T(8,128)(2,1)S(1)} %slice.468), channel_id=1, source_target_pairs={{0,8},{1,9},{2,10},{3,11},{4,12},{5,13},{6,14},{7,15},{8,0},{9,1},... | collective-permute-start | bytes 1572872 | tf_op jit(solution)/shard_map/ppermute | solution.py:704
  276.6 28.0 %collective-permute-start.42 = (bf16[512,256]{1,0:T(8,128)(2,1)S(1)}, bf16[512,256]{1,0:T(8,128)(2,1)S(1)}, u32[]{:S(2)}, u32[]{:S(2)}) collective-permute-start(bf16[512,256]{1,0:T(8,128)(2,1)S(1)} %slice.472), channel_id=1, source_target_pairs={{0,4},{1,3},{2,6},{3,1},{4,0},{5,7},{6,2},{7,5},{8,12},{9,11},{10,... | collective-permute-start | bytes 786440 | tf_op jit(solution)/shard_map/ppermute | solution.py:704
  280.7 26.6 %collective-permute-start.48 = (bf16[512,256]{1,0:T(8,128)(2,1)S(1)}, bf16[512,256]{1,0:T(8,128)(2,1)S(1)}, u32[]{:S(2)}, u32[]{:S(2)}) collective-permute-start(bf16[512,256]{1,0:T(8,128)(2,1)S(1)} %slice.471), channel_id=1, source_target_pairs={{0,4},{1,3},{2,6},{3,1},{4,0},{5,7},{6,2},{7,5},{8,12},{9,11},{10,... | collective-permute-start | bytes 786440 | tf_op jit(solution)/shard_map/ppermute | solution.py:704
  292.0 15.8 %collective-permute-start.30 = (bf16[128,1024]{1,0:T(8,128)(2,1)S(1)}, bf16[128,1024]{1,0:T(8,128)(2,1)S(1)}, u32[]{:S(2)}, u32[]{:S(2)}) collective-permute-start(bf16[128,1024]{1,0:T(8,128)(2,1)S(1)} %slice.474), channel_id=1, source_target_pairs={{0,4},{1,3},{2,6},{3,1},{4,0},{5,7},{6,2},{7,5},{8,12},{9,11},{10,... | collective-permute-start | bytes 786440 | tf_op jit(solution)/shard_map/ppermute | solution.py:704
  302.2 8.3 %collective-permute-start.36 = (bf16[128,1024]{1,0:T(8,128)(2,1)S(1)}, bf16[128,1024]{1,0:T(8,128)(2,1)S(1)}, u32[]{:S(2)}, u32[]{:S(2)}) collective-permute-start(bf16[128,1024]{1,0:T(8,128)(2,1)S(1)} %slice.473), channel_id=1, source_target_pairs={{0,4},{1,3},{2,6},{3,1},{4,0},{5,7},{6,2},{7,5},{8,12},{9,11},{10,... | collective-permute-start | bytes 786440 | tf_op jit(solution)/shard_map/ppermute | solution.py:704
  304.3 26.5 %collective-permute-start.11 = (bf16[256,1024]{1,0:T(8,128)(2,1)S(1)}, bf16[256,1024]{1,0:T(8,128)(2,1)S(1)}, u32[]{:S(2)}, u32[]{:S(2)}) collective-permute-start(bf16[256,1024]{1,0:T(8,128)(2,1)S(1)} %slice.470), channel_id=1, source_target_pairs={{0,8},{1,9},{2,10},{3,11},{4,12},{5,13},{6,14},{7,15},{8,0},{9,1},... | collective-permute-start | bytes 1572872 | tf_op jit(solution)/shard_map/ppermute | solution.py:704
  304.7 15.2 %collective-permute-start.43 = (bf16[256,256]{1,0:T(8,128)(2,1)S(1)}, bf16[256,256]{1,0:T(8,128)(2,1)S(1)}, u32[]{:S(2)}, u32[]{:S(2)}) collective-permute-start(bf16[256,256]{1,0:T(8,128)(2,1)S(1)} %slice.479), channel_id=1, source_target_pairs={{0,16},{1,17},{2,18},{3,19},{4,20},{5,21},{6,22},{7,23},{8,24},{9,... | collective-permute-start | bytes 393224 | tf_op jit(solution)/shard_map/ppermute | solution.py:704
  307.4 15.3 %collective-permute-start.49 = (bf16[256,256]{1,0:T(8,128)(2,1)S(1)}, bf16[256,256]{1,0:T(8,128)(2,1)S(1)}, u32[]{:S(2)}, u32[]{:S(2)}) collective-permute-start(bf16[256,256]{1,0:T(8,128)(2,1)S(1)} %slice.478), channel_id=1, source_target_pairs={{0,16},{1,17},{2,18},{3,19},{4,20},{5,21},{6,22},{7,23},{8,24},{9,... | collective-permute-start | bytes 393224 | tf_op jit(solution)/shard_map/ppermute | solution.py:704
  308.0 16.8 %collective-permute-start.31 = (bf16[64,1024]{1,0:T(8,128)(2,1)S(1)}, bf16[64,1024]{1,0:T(8,128)(2,1)S(1)}, u32[]{:S(2)}, u32[]{:S(2)}) collective-permute-start(bf16[64,1024]{1,0:T(8,128)(2,1)S(1)} %slice.481), channel_id=1, source_target_pairs={{0,16},{1,17},{2,18},{3,19},{4,20},{5,21},{6,22},{7,23},{8,24},{9,... | collective-permute-start | bytes 393224 | tf_op jit(solution)/shard_map/ppermute | solution.py:704
  310.6 18.8 %collective-permute-start.37 = (bf16[64,1024]{1,0:T(8,128)(2,1)S(1)}, bf16[64,1024]{1,0:T(8,128)(2,1)S(1)}, u32[]{:S(2)}, u32[]{:S(2)}) collective-permute-start(bf16[64,1024]{1,0:T(8,128)(2,1)S(1)} %slice.480), channel_id=1, source_target_pairs={{0,16},{1,17},{2,18},{3,19},{4,20},{5,21},{6,22},{7,23},{8,24},{9,... | collective-permute-start | bytes 393224 | tf_op jit(solution)/shard_map/ppermute | solution.py:704
  319.9 13.1 %collective-permute-start.44 = (bf16[128,256]{1,0:T(8,128)(2,1)S(1)}, bf16[128,256]{1,0:T(8,128)(2,1)S(1)}, u32[]{:S(2)}, u32[]{:S(2)}) collective-permute-start(bf16[128,256]{1,0:T(8,128)(2,1)S(1)} %slice.486), channel_id=1, source_target_pairs={{0,1},{1,0},{2,3},{3,2},{4,5},{5,4},{6,7},{7,6},{8,9},{9,8},{10,11... | collective-permute-start | bytes 196616 | tf_op jit(solution)/shard_map/ppermute | solution.py:704
  322.7 15.1 %collective-permute-start.50 = (bf16[128,256]{1,0:T(8,128)(2,1)S(1)}, bf16[128,256]{1,0:T(8,128)(2,1)S(1)}, u32[]{:S(2)}, u32[]{:S(2)}) collective-permute-start(bf16[128,256]{1,0:T(8,128)(2,1)S(1)} %slice.485), channel_id=1, source_target_pairs={{0,1},{1,0},{2,3},{3,2},{4,5},{5,4},{6,7},{7,6},{8,9},{9,8},{10,11... | collective-permute-start | bytes 196616 | tf_op jit(solution)/shard_map/ppermute | solution.py:704
  324.8 4.7 %collective-permute-start.32 = (bf16[32,1024]{1,0:T(8,128)(2,1)S(1)}, bf16[32,1024]{1,0:T(8,128)(2,1)S(1)}, u32[]{:S(2)}, u32[]{:S(2)}) collective-permute-start(bf16[32,1024]{1,0:T(8,128)(2,1)S(1)} %slice.488), channel_id=1, source_target_pairs={{0,1},{1,0},{2,3},{3,2},{4,5},{5,4},{6,7},{7,6},{8,9},{9,8},{10,11... | collective-permute-start | bytes 196616 | tf_op jit(solution)/shard_map/ppermute | solution.py:704
  331.0 6.4 %collective-permute-start.12 = (bf16[128,1024]{1,0:T(8,128)(2,1)S(1)}, bf16[128,1024]{1,0:T(8,128)(2,1)S(1)}, u32[]{:S(2)}, u32[]{:S(2)}) collective-permute-start(bf16[128,1024]{1,0:T(8,128)(2,1)S(1)} %slice.477), channel_id=1, source_target_pairs={{0,4},{1,3},{2,6},{3,1},{4,0},{5,7},{6,2},{7,5},{8,12},{9,11},{10,... | collective-permute-start | bytes 786440 | tf_op jit(solution)/shard_map/ppermute | solution.py:704
  337.5 8.4 %collective-permute-start.13 = (bf16[64,1024]{1,0:T(8,128)(2,1)S(1)}, bf16[64,1024]{1,0:T(8,128)(2,1)S(1)}, u32[]{:S(2)}, u32[]{:S(2)}) collective-permute-start(bf16[64,1024]{1,0:T(8,128)(2,1)S(1)} %slice.484), channel_id=1, source_target_pairs={{0,16},{1,17},{2,18},{3,19},{4,20},{5,21},{6,22},{7,23},{8,24},{9,... | collective-permute-start | bytes 393224 | tf_op jit(solution)/shard_map/ppermute | solution.py:704
  (44 other events, 327.9 us)
